TPU v7x, 32 devices: a whole 2x2x4 slice. The times are simulated.
32 devices in a mesh: section: 2 (over core), dp: 8 (over z, y), mp: 2 (over x).
Axes of the slice: x: 2, y: 2, z: 4, core: 2. Of those that a mesh axis runs over, the one named last changes fastest.
Arguments:
- qkv: bfloat16 [1024, 3072], P('dp', ('section', 'mp')), may hold values from -6 to 6
- kv_cache: bfloat16 [512, 8, 2048], P('dp', None, ('section', 'mp')), may hold values from -6 to 6
- residual: bfloat16 [1024, 2048], P('dp'), may hold values from -6 to 6
- out_weight: bfloat16 [1024, 2048], P(('section', 'mp')), may hold values from -0.1875 to 0.1875
- moe_gain: float32 [2048], replicated, may hold values from 0.1 to 1.9
- w_gate: bfloat16 [8, 2048, 1408], P('dp', None, ('section', 'mp')), may hold values from -0.125 to 0.125
- w_up: bfloat16 [8, 2048, 1408], P('dp', None, ('section', 'mp')), may hold values from -0.125 to 0.125
- w_down: bfloat16 [8, 1408, 2048], P('dp', ('section', 'mp')), may hold values from -0.15625 to 0.15625
- seg_ids: int32 [8, 1, 128], P('dp'), may hold values from 0 to 3, never falling along the last dimension, each value on 1 to 64 neighbouring positions
- prefix_blocks: int32 [8, 1, 4], P('dp'), may hold values from 1 to 32, 64 in all within a row
- owners: int32 [8, 1, 64, 1], replicated, may hold values from 0 to 7; in each aligned block of 64 rows (0 to 63, 64 to 127, ..., all dimensions but the last counted through in order) at most 24 rows name the same one
- slot_ids: int32 [8, 1, 64], replicated, may hold values from 0 to 63
- expert_ids: int32 [1024, 4], P('dp'), may hold values from 0 to 7, all different within a row; in each aligned block of 32 rows (0 to 31, 32 to 63, ...) at most 32 rows name the same one
- gate_weights: float32 [1024, 4], P('dp'), may hold values from 0.05 to 0.5
Outputs:
- layer_out: bfloat16 [1024, 2048], P('dp', ('section', 'mp'))
Inputs may be any that keep to these rules, and one draw needn't show every extreme that they name: seg_ids[g, m] never falls along the tokens; each of the 4 requests has 1 to 64 tokens, one exactly 64. `prefix_blocks`: the 4 counts of each (g, m) sum to 64, one of them is 32. `owners`: in each block table of 64 entries no owner appears more than 24 times, and some owner appears exactly 24 times in some table. `expert_ids`: each token names 4 different experts; in each aligned block of 32 tokens no expert is named by more than 32 tokens, a bound that some block reaches.
All inputs are finite; a program needn't handle non-finite values.
Results may differ from a plain program's by a relative error of at most 0.009.
Values may be sent and summed in bfloat16 or wider, within the bound.
A program may use at most 64 MiB of HBM per device.

v0:
```python
import math

import jax
import jax.numpy as jnp
from jax import lax
from jax.sharding import PartitionSpec as P

HEAD_DIM = 128
TOPK = 4
PREF = 64
BLK = 8


def normalize(hidden, gain):
    square = jnp.mean(hidden * hidden, axis=-1, keepdims=True)
    return (hidden * lax.rsqrt(square + 1e-06) * gain).astype(jnp.bfloat16)


def expert_rows(inputs, w_gate, w_up, w_down):
    model_width = inputs.shape[-1]
    flat_rows = inputs.reshape(-1, model_width)
    gate_rows = jnp.dot(flat_rows, w_gate[0], preferred_element_type=jnp.float32)
    up_rows = jnp.dot(flat_rows, w_up[0], preferred_element_type=jnp.float32)
    hidden = (jax.nn.silu(gate_rows) * up_rows).astype(jnp.bfloat16)
    result = jnp.dot(hidden, w_down[0], preferred_element_type=jnp.float32).astype(jnp.bfloat16)
    return result.reshape(inputs.shape[:-1] + (result.shape[-1],))


def slot_table(pair_ids, pair_slots, experts, capacity):
    pair_count = pair_ids.shape[0]
    expert_match = pair_ids[None, None, :] == jnp.arange(experts, dtype=jnp.int32)[:, None, None]
    slot_match = pair_slots[None, None, :] == jnp.arange(capacity, dtype=jnp.int32)[None, :, None]
    pair_match = expert_match & slot_match
    token_of = jnp.arange(pair_count, dtype=jnp.int32) // TOPK
    source = jnp.sum(jnp.where(pair_match, token_of[None, None, :], 0), axis=2)
    filled = jnp.any(pair_match, axis=2)
    return (source, filled)


def dispatch_rows(normed, source, filled):
    gathered = jnp.take(normed, source.reshape(-1), axis=0).reshape(
        source.shape + (normed.shape[-1],)
    )
    return jnp.where(filled[:, :, None], gathered, jnp.zeros_like(gathered))


def local(
    qkv,
    kv_cache,
    residual,
    out_weight,
    moe_gain,
    w_gate,
    w_up,
    w_down,
    seg_ids,
    prefix_blocks,
    owners,
    slot_ids,
    expert_ids,
    gate_weights,
):
    groups = lax.axis_size("dp")
    shards = lax.axis_size("section") * lax.axis_size("mp")
    group_index = lax.axis_index("dp")
    shard_index = lax.axis_index("section") * lax.axis_size("mp") + lax.axis_index("mp")
    mb_rows = seg_ids.shape[2]
    quarter_rows = mb_rows // shards
    model_width = residual.shape[1]
    part_cols = model_width // shards
    head_cols = out_weight.shape[0]
    heads_local = head_cols // HEAD_DIM
    cache_cols = kv_cache.shape[2]
    quarter_cap = min(quarter_rows, max(2, 2 * quarter_rows * TOPK // groups))
    capacity = shards * quarter_cap
    owner_cap = max(3, 3 * PREF // groups)
    score_scale = 1.0 / math.sqrt(HEAD_DIM)
    own_table = owners[:, 0, :, 0]
    slot_table_m = slot_ids[:, 0, :]
    owned_here = own_table == group_index
    local_order = jnp.cumsum(owned_here.astype(jnp.int32), axis=1) - 1
    wanted = owned_here[:, None, :] & (
        local_order[:, None, :] == jnp.arange(owner_cap, dtype=jnp.int32)[None, :, None]
    )
    slot_pick = jnp.sum(jnp.where(wanted, slot_table_m[:, None, :], 0), axis=2)
    filled = jnp.any(wanted, axis=2)
    chosen = jnp.take(kv_cache, slot_pick.reshape(-1), axis=0).reshape(
        groups, owner_cap, BLK, cache_cols
    )
    chosen = jnp.where(filled[:, :, None, None], chosen, jnp.zeros_like(chosen))
    arrived = lax.all_to_all(chosen, "dp", split_axis=0, concat_axis=0, tiled=True)
    my_owner = lax.dynamic_index_in_dim(own_table, group_index, 0, keepdims=False)
    block_index = jnp.arange(PREF, dtype=jnp.int32)
    earlier = (my_owner[None, :] == my_owner[:, None]) & (
        block_index[None, :] < block_index[:, None]
    )
    my_rank = jnp.sum(earlier.astype(jnp.int32), axis=1)
    where_from = my_owner * owner_cap + my_rank
    prefix = jnp.take(arrived.reshape(groups * owner_cap, BLK, cache_cols), where_from, axis=0)
    prefix = prefix.reshape(PREF * BLK, heads_local, 2, HEAD_DIM)
    tokens = qkv
    tokens = tokens.reshape(mb_rows, heads_local, 3, HEAD_DIM)
    query_rows = tokens[:, :, 0]
    key_rows = jnp.concatenate([prefix[:, :, 0], tokens[:, :, 1]], axis=0)
    value_rows = jnp.concatenate([prefix[:, :, 1], tokens[:, :, 2]], axis=0)
    segments = seg_ids[0, 0]
    block_ends = jnp.cumsum(prefix_blocks[0, 0])
    block_seg = jnp.sum((block_ends[None, :] <= block_index[:, None]).astype(jnp.int32), axis=1)
    prefix_seg = jnp.repeat(block_seg, BLK)
    position = jnp.arange(mb_rows, dtype=jnp.int32)
    same_prefix = prefix_seg[None, :] == segments[:, None]
    same_new = (segments[None, :] == segments[:, None]) & (position[None, :] <= position[:, None])
    visible = jnp.concatenate([same_prefix, same_new], axis=1)
    scores = (
        jnp.einsum("qhd,khd->hqk", query_rows, key_rows, preferred_element_type=jnp.float32)
        * score_scale
    )
    scores = jnp.where(visible[None], scores, -jnp.inf)
    row_max = jnp.max(scores, axis=2, keepdims=True)
    weights = jnp.exp(scores - row_max)
    attention = (weights / jnp.sum(weights, axis=2, keepdims=True)).astype(jnp.bfloat16)
    combined = jnp.einsum("hqk,khd->qhd", attention, value_rows, preferred_element_type=jnp.float32)
    attended_now = combined.astype(jnp.bfloat16).reshape(mb_rows, head_cols)
    stream = residual.astype(jnp.float32)
    projected = jnp.dot(attended_now, out_weight, preferred_element_type=jnp.float32)
    quarter_ids = expert_ids.reshape(shards, quarter_rows * TOPK)
    one_hot = (
        quarter_ids[:, :, None] == jnp.arange(groups, dtype=jnp.int32)[None, None, :]
    ).astype(jnp.int32)
    quarter_rank = jnp.sum((jnp.cumsum(one_hot, axis=1) - one_hot) * one_hot, axis=2)
    flat_ids = expert_ids.reshape(-1)
    flat_slot = (quarter_rank + jnp.arange(shards, dtype=jnp.int32)[:, None] * quarter_cap).reshape(
        -1
    )
    mixed_in = stream + lax.psum(projected, ("section", "mp"))
    normed = normalize(mixed_in, moe_gain)
    source, filled = slot_table(flat_ids, flat_slot, groups, capacity)
    outgoing = dispatch_rows(normed, source, filled)
    incoming = lax.all_to_all(outgoing, "dp", split_axis=0, concat_axis=0, tiled=True)
    produced = expert_rows(incoming, w_gate, w_up, w_down)
    returned = lax.all_to_all(produced, "dp", split_axis=0, concat_axis=0, tiled=True)
    position = flat_ids * capacity + flat_slot
    picked = jnp.take(returned.reshape(groups * capacity, model_width), position, axis=0)
    picked = picked.reshape(mb_rows, TOPK, model_width)
    weighted = jnp.einsum("tk,tkd->td", gate_weights, picked.astype(jnp.float32))
    moe_full = lax.psum(weighted.astype(jnp.bfloat16), ("section", "mp")).astype(jnp.float32)
    finished = (mixed_in + moe_full).astype(jnp.bfloat16).reshape(mb_rows, shards, part_cols)
    return lax.dynamic_index_in_dim(finished, shard_index, 1, keepdims=False)


def solution(mesh):
    return jax.shard_map(
        local,
        mesh=mesh,
        in_specs=(
            P("dp", ("section", "mp")),
            P("dp", None, ("section", "mp")),
            P("dp", None),
            P(("section", "mp"), None),
            P(),
            P("dp", None, ("section", "mp")),
            P("dp", None, ("section", "mp")),
            P("dp", ("section", "mp"), None),
            P("dp", None, None),
            P("dp", None, None),
            P(),
            P(),
            P("dp", None),
            P("dp", None),
        ),
        out_specs=P("dp", ("section", "mp")),
        check_vma=False,
    )
```

profile of v0, /device:TPU:1, one launch (start us, length us, event | category | flops | bytes accessed | tf_op | source)
XLA Modules:
  0.0 374.1 jit_solution(3808025803328037853)
XLA Ops:
  6.5 0.8 broadcast_compare_fusion.1
  7.4 0.2 reduce_window_sum.29
  7.6 0.9 select_reduce_fusion.1
  8.6 0.2 fusion.28
  8.8 1.9 gather_fusion
  10.8 1.5 select_select_fusion.1
  12.3 6.5 %all-to-all-start = ((bf16[8,24,8,512]{3,2,1,0:T(8,128)(2,1)}), bf16[8,24,8,512]{3,2,1,0:T(8,128)(2,1)S(1)}, u32[]{:S(2)}, u32[]{:S(2)}) async-start(bf16[8,24,8,512]{3,2,1,0:T(8,128)(2,1)} %select_select_fusion.1), calls=%async_computation | async-start | bytes 3145728 | tf_op jit(solution)/shard_map/all_to_all | solution.py:91
  18.8 0.7 fusion.39
  19.5 0.2 convert_reduce_fusion
  19.7 0.2 copy.41
  19.9 0.6 copy-done.7
  20.5 0.7 compare_and_fusion.3
  21.2 0.1 copy.47
  21.3 0.1 eq.143
  21.4 0.1 eq.147
  21.6 0.6 broadcast_in_dim.131
  22.2 0.7 copy.59
  22.9 0.2 reduce-window.8
  23.4 0.7 copy.58
  24.1 0.1 fusion.26
  24.2 0.3 reduce_window_sum.30
  24.5 0.7 fusion.36
  25.2 0.6 pad_clamp_fusion.1
  25.8 0.8 fusion.29
  26.6 0.8 broadcast_compare_fusion
  27.4 0.6 pad_add_fusion
  28.1 0.2 select_reduce_fusion
  28.5 0.4 fusion.1
  28.8 0.2 copy-done.5
  29.1 0.6 compare_and_fusion
  29.6 25.3 %all-to-all-done = bf16[8,24,8,512]{3,2,1,0:T(8,128)(2,1)S(1)} async-done(((bf16[8,24,8,512]{3,2,1,0:T(8,128)(2,1)}), bf16[8,24,8,512]{3,2,1,0:T(8,128)(2,1)S(1)}, u32[]{:S(2)}, u32[]{:S(2)}) %all-to-all-start) | async-done | bytes 1572896 | tf_op jit(solution)/shard_map/all_to_all | solution.py:91
  54.9 0.7 gather_fusion.1
  55.7 0.1 gather.27
  55.8 0.7 copy_select_fusion
  56.6 1.1 fusion.15
  57.7 0.4 fusion.49
  58.1 1.8 convolution_convert_fusion.1
  59.9 1.4 fusion.52
  61.3 0.8 and_reduce_fusion
  62.1 35.4 %all-reduce.3.cloned.1.call-done = f32[128,2048]{1,0:T(8,128)} async-done(((f32[128,2048]{1,0:T(8,128)}), f32[128,2048]{1,0:T(8,128)}) %all-reduce.3.cloned.1.call-update) | async-done | bytes 1048592 | tf_op jit(solution)/shard_map/psum | solution.py:135
  97.5 1.5 multiply_reduce_fusion
  99.1 0.9 multiply_convert_fusion
  100.0 6.0 %gather_fusion.2 = bf16[1024,2048]{1,0:T(8,128)(2,1)} fusion(bf16[128,2048]{1,0:T(8,128)(2,1)S(1)} %multiply_convert_fusion, s32[1024]{0:T(1024)S(1)} %broadcast_clamp_fusion), kind=kCustom, calls=%fused_computation.2 | custom fusion | bytes 8392704 | tf_op jit(solution)/shard_map/jit(_take)/gather | solution.py:41
  106.0 2.6 select_select_fusion
  108.6 97.3 %all_to_all.15 = bf16[8,128,2048]{2,1,0:T(8,128)(2,1)S(1)} all-to-all(bf16[8,128,2048]{2,1,0:T(8,128)(2,1)S(1)} %select_select_fusion), channel_id=1, replica_groups=mesh['section'=2,'dp'=8,'mp'=2] {'dp'}, dimensions={0} | all-to-all | bytes 8388608 | tf_op jit(solution)/shard_map/all_to_all | solution.py:139
  205.9 2.0 copy-done.3
  207.9 2.9 fusion.7
  210.8 9.0 %convolution_convert_fusion = bf16[1024,2048]{1,0:T(8,128)(2,1)} fusion(bf16[1,352,2048]{2,1,0:T(8,128)(2,1)S(1)} %copy-done, bf16[1024,2048]{1,0:T(8,128)(2,1)} %bitcast.88, bf16[1,2048,352]{1,2,0:T(8,128)(2,1)} %param.20, f32[1024,352]{0,1:T(8,128)} %fusion.7), kind=kOutput, calls=%fused_computation.6 | convolution fusion | flops 2957049856 | bytes 12713984 | tf_op jit(solution)/shard_map/dot_general | solution.py:25
  219.7 4.7 %all-to-all-start.2 = ((bf16[8,128,2048]{2,1,0:T(8,128)(2,1)}), bf16[8,128,2048]{2,1,0:T(8,128)(2,1)}, u32[]{:S(2)}, u32[]{:S(2)}) async-start(bf16[8,128,2048]{2,1,0:T(8,128)(2,1)} %bitcast.86), calls=%async_computation.2 | async-start | bytes 8388608 | tf_op jit(solution)/shard_map/all_to_all | solution.py:141
  224.4 0.2 all-reduce.5.cloned.1.call-start
  224.8 0.1 copy.51
  224.9 0.1 mul.111
  225.3 0.1 copy.49
  225.4 0.2 copy.55
  225.7 90.1 %all-to-all-done.2 = bf16[8,128,2048]{2,1,0:T(8,128)(2,1)} async-done(((bf16[8,128,2048]{2,1,0:T(8,128)(2,1)}), bf16[8,128,2048]{2,1,0:T(8,128)(2,1)}, u32[]{:S(2)}, u32[]{:S(2)}) %all-to-all-start.2) | async-done | bytes 4194336 | tf_op jit(solution)/shard_map/all_to_all | solution.py:141
  315.7 8.0 %gather_fusion.3 = bf16[512,2048]{1,0:T(8,128)(2,1)} fusion(bf16[1024,2048]{1,0:T(8,128)(2,1)} %bitcast.29, s32[1024]{0:T(1024)S(1)} %pad_clamp_fusion), kind=kCustom, calls=%fused_computation.3 | custom fusion | bytes 4196352 | tf_op jit(solution)/shard_map/jit(_take)/gather | solution.py:143
  323.8 4.1 %gather.31 = bf16[128,4,2048]{2,1,0:T(4,128)(2,1)} reshape(bf16[512,2048]{1,0:T(8,128)(2,1)} %gather_fusion.3) | data formatting | bytes 4194304 | tf_op jit(solution)/shard_map/jit(_take)/gather | solution.py:143
  327.9 2.9 fusion.2
  330.8 1.1 copy.67
  331.9 32.7 %all-reduce.5.cloned.1.call-done = bf16[128,2048]{1,0:T(8,128)(2,1)} async-done(((bf16[128,2048]{1,0:T(8,128)(2,1)}), bf16[128,2048]{1,0:T(8,128)(2,1)}) %all-reduce.5.cloned.1.call-update) | async-done | bytes 524304 | tf_op jit(solution)/shard_map/psum | solution.py:146
  364.6 1.2 add_convert_fusion
  365.9 0.4 reshape.362
  366.3 0.3 constant_dynamic-slice_fusion
  366.5 0.7 copy.68
  (71 shorter events, 1.3 us)
Async XLA Ops:
  6.5 204.2 %copy-start = (bf16[1,352,2048]{2,1,0:T(8,128)(2,1)S(1)}, bf16[1,352,2048]{2,1,0:T(8,128)(2,1)}, u32[]{:S(2)}) copy-start(bf16[1,352,2048]{2,1,0:T(8,128)(2,1)} %param.21) | copy-start | bytes 4325380
  12.3 7.4 %copy-start.9 = (bf16[128,768]{1,0:T(8,128)(2,1)S(1)}, bf16[128,768]{1,0:T(8,128)(2,1)}, u32[]{:S(2)}) copy-start(bf16[128,768]{1,0:T(8,128)(2,1)} %param.14) | copy-start | bytes 589828
  12.3 8.9 %copy-start.13 = (s32[128,4]{0,1:T(4,128)S(1)}, s32[128,4]{0,1:T(4,128)}, u32[]{:S(2)}) copy-start(s32[128,4]{0,1:T(4,128)} %param.26) | copy-start | bytes 6148
  12.3 10.7 %copy-start.20 = (s32[1,1,4]{2,1,0:T(1,128)S(1)}, s32[1,1,4]{2,1,0:T(1,128)}, u32[]{:S(2)}) copy-start(s32[1,1,4]{2,1,0:T(1,128)} %param.23) | copy-start | bytes 52
  12.3 42.7 %all-to-all-start = ((bf16[8,24,8,512]{3,2,1,0:T(8,128)(2,1)}), bf16[8,24,8,512]{3,2,1,0:T(8,128)(2,1)S(1)}, u32[]{:S(2)}, u32[]{:S(2)}) async-start(bf16[8,24,8,512]{3,2,1,0:T(8,128)(2,1)} %select_select_fusion.1), calls=%async_computation | async-start | bytes 3145728 | tf_op jit(solution)/shard_map/all_to_all | solution.py:91
  18.8 78.7 %all-reduce.3.cloned.1.call-start = ((), (), s32[]{:S(2)}) async-start(), calls=%async_computation.3 | async-start | bytes 2097152 | tf_op jit(solution)/shard_map/psum | solution.py:135
  19.7 3.7 copy-start.18
  19.9 0.7 copy-start.7
  24.5 30.4 %copy-start.14 = (s32[4]{0:T(128)}, s32[4]{0:T(128)S(1)}, u32[]{:S(2)}) copy-start(s32[4]{0:T(128)S(1)} %iota_multiply_fusion) | copy-start | bytes 52
  28.4 0.6 copy-start.5
  55.6 0.9 copy-start.8
  55.7 1.0 copy-start.10
  55.7 1.0 copy-start.11
  56.5 1.6 copy-start.12
  58.1 1.8 copy-start.4
  59.9 1.4 copy-start.6
  59.9 37.7 %copy-start.2 = (bf16[128,2048]{1,0:T(8,128)(2,1)S(1)}, bf16[128,2048]{1,0:T(8,128)(2,1)}, u32[]{:S(2)}) copy-start(bf16[128,2048]{1,0:T(8,128)(2,1)} %param.16) | copy-start | bytes 1572868
  97.5 1.5 copy-start.1
  99.9 6.0 %copy-start.16 = (pred[8,128]{1,0:T(8,128)(4,1)S(1)}, pred[8,128]{1,0:T(8,128)(4,1)}, u32[]{:S(2)}) copy-start(pred[8,128]{1,0:T(8,128)(4,1)} %and_reduce_fusion) | copy-start | bytes 3076
  108.6 99.3 %copy-start.19 = (bf16[1,2048,352]{1,2,0:T(8,128)(2,1)S(1)}, bf16[1,2048,352]{1,2,0:T(8,128)(2,1)}, u32[]{:S(2)}) copy-start(bf16[1,2048,352]{1,2,0:T(8,128)(2,1)} %param.19) | copy-start | bytes 4325380
  205.9 2.0 copy-start.3
  219.7 5.3 %copy-start.15 = (s32[4]{0:T(128)S(1)}, s32[4]{0:T(128)}, u32[]{:S(2)}) copy-start(s32[4]{0:T(128)} %copy-done.14) | copy-start | bytes 52
  219.7 5.7 %copy-start.17 = (f32[128,4]{0,1:T(4,128)S(1)}, f32[128,4]{0,1:T(4,128)}, u32[]{:S(2)}) copy-start(f32[128,4]{0,1:T(4,128)} %param.27) | copy-start | bytes 6148
  219.7 96.0 %all-to-all-start.2 = ((bf16[8,128,2048]{2,1,0:T(8,128)(2,1)}), bf16[8,128,2048]{2,1,0:T(8,128)(2,1)}, u32[]{:S(2)}, u32[]{:S(2)}) async-start(bf16[8,128,2048]{2,1,0:T(8,128)(2,1)} %bitcast.86), calls=%async_computation.2 | async-start | bytes 8388608 | tf_op jit(solution)/shard_map/all_to_all | solution.py:141
  224.4 140.2 %all-reduce.5.cloned.1.call-start = ((), (), s32[]{:S(2)}) async-start(), calls=%async_computation.4 | async-start | bytes 1048576 | tf_op jit(solution)/shard_map/psum | solution.py:146
Sparse Core Ops, SparseCore 0:
  61.4 36.0 all-reduce.2
  332.1 32.5 all-reduce.4
where the time goes:
time: 377 us; the launch traced here: 374 us
  waiting for transfers between devices  183 us (49%)
  blocking collectives  97.3 us (26%)
  local copies, waits for them, and re-layouts  30.8 us (8%)
  matrix products  19.3 us (5%)
  other arithmetic  17.8 us (5%)
  between operations  13.8 us (4%)
  starting transfers between devices  11.5 us (3%)
    all_to_all x1, blocking collectives, local(): lax.all_to_all(outgoing, 'dp', split_axis=0, concat_axis=0, tiled=True)  97.3 us
    all_to_all x1, waiting for transfers between devices, local(): lax.all_to_all(produced, 'dp', split_axis=0, concat_axis=0, tiled=True)  90.1 us
    psum x1, waiting for transfers between devices, local(): mixed_in = stream + lax.psum(projected, ('section', 'mp'))  35.4 us
    psum x1, waiting for transfers between devices, local(): lax.psum(weighted.astype(jnp.bfloat16), ('section', 'mp'))  32.7 us
    all_to_all x1, waiting for transfers between devices, local(): lax.all_to_all(chosen, 'dp', split_axis=0, concat_axis=0, tiled=True)  25.3 us
    gather x2, local copies, waits for them, and re-layouts, local(): jnp.take(returned.reshape(groups * capacity, model_width), position, axis=0)  12.1 us
    dot_general x1, matrix products, expert_rows(): jnp.dot(hidden, w_down[0], preferred_element_type=jnp.float32)  8.96 us
  transfers between devices with their start and end apart: 4, of which 4 were waited for; matrix products, arithmetic and copies ran while one was open for 3% of the time, Pallas kernels for 0%

commit v1 on v0

--- a/solution.py
+++ b/solution.py
@@ -1,14 +1,20 @@
 import math
+from functools import partial
 
 import jax
 import jax.numpy as jnp
 from jax import lax
+from jax.experimental import pallas as pl
+from jax.experimental.pallas import tpu as pltpu
 from jax.sharding import PartitionSpec as P
 
 HEAD_DIM = 128
 TOPK = 4
 PREF = 64
 BLK = 8
+MESH = pl.DeviceIdType.MESH
+DENSE_GROUPS = 8
+NEG = -1e30
 
 
 def normalize(hidden, gain):
@@ -44,7 +50,7 @@
     return jnp.where(filled[:, :, None], gathered, jnp.zeros_like(gathered))
 
 
-def local(
+def local_sparse(
     qkv,
     kv_cache,
     residual,
@@ -148,9 +154,489 @@
     return lax.dynamic_index_in_dim(finished, shard_index, 1, keepdims=False)
 
 
+def remote(src, dst, send, recv, device):
+    return pltpu.make_async_remote_copy(
+        src_ref=src, dst_ref=dst, send_sem=send, recv_sem=recv, device_id=device, device_id_type=MESH
+    )
+
+
+def contract_last(a, b):
+    return lax.dot_general(a, b, (((1,), (1,)), ((), ())), preferred_element_type=jnp.float32)
+
+
+def layer_kernel(
+    groups,
+    qkv_ref,
+    kv_ref,
+    res_ref,
+    ow_ref,
+    gain_ref,
+    wg_hbm,
+    wu_hbm,
+    wd_hbm,
+    meta_ref,
+    table_ref,
+    cw_ref,
+    out_ref,
+    wg,
+    wu,
+    wd,
+    qb,
+    mb,
+    os,
+    orv,
+    mls,
+    mlr,
+    ps,
+    pr,
+    ss,
+    nb,
+    xb,
+    yown,
+    ys,
+    yr,
+    rs,
+    rb,
+    mixed,
+    w_local,
+    w_send,
+    w_recv,
+    q_send,
+    q_recv,
+    m_send,
+    m_recv,
+    o_send,
+    o_recv,
+    l_send,
+    l_recv,
+    p_send,
+    p_recv,
+    s_send,
+    s_recv,
+    x_send,
+    x_recv,
+    f_send,
+    y_send,
+    y_recv,
+    r_send,
+    r_recv,
+):
+    s = lax.axis_index("section")
+    g = lax.axis_index("dp")
+    m = lax.axis_index("mp")
+    q = s * 2 + m
+    rows = qkv_ref.shape[0]
+    wide = out_ref.shape[1]
+    half = groups // 2
+    scale = 1.0 / math.sqrt(HEAD_DIM)
+    core_peer = (1 - s, g, m)
+    x_peer = (s, g, 1 - m)
+
+    barrier = pltpu.get_barrier_semaphore()
+
+    def greet(k, carry):
+        other = lax.rem(s * groups + g + k, 2 * groups)
+        pl.semaphore_signal(
+            barrier, inc=1, device_id=(other // groups, lax.rem(other, groups), m), device_id_type=MESH
+        )
+        return carry
+
+    lax.fori_loop(1, 2 * groups, greet, 0)
+    pl.semaphore_signal(barrier, inc=1, device_id=x_peer, device_id_type=MESH)
+    pl.semaphore_signal(barrier, inc=1, device_id=(1 - s, g, 1 - m), device_id_type=MESH)
+
+    for h in range(2):
+        qb[g, :, h * HEAD_DIM : (h + 1) * HEAD_DIM] = qkv_ref[:, h * 3 * HEAD_DIM : h * 3 * HEAD_DIM + HEAD_DIM]
+    mb[g] = meta_ref[...]
+    pl.semaphore_wait(barrier, 2 * groups + 1)
+
+    def send_query(k, carry):
+        to = (s, lax.rem(g + k, groups), m)
+        remote(mb.at[g], mb.at[g], m_send.at[k], m_recv.at[g], to).start()
+        remote(qb.at[g], qb.at[g], q_send.at[k], q_recv.at[g], to).start()
+        return carry
+
+    lax.fori_loop(1, groups, send_query, 0)
+
+    weights = ((wg_hbm, wg), (wu_hbm, wu), (wd_hbm, wd))
+    for i, (hbm, vmem) in enumerate(weights):
+        pltpu.make_async_copy(hbm.at[0], vmem.at[s], w_local.at[i]).start()
+        remote(hbm.at[0], vmem.at[s], w_send.at[i], w_recv.at[i], core_peer).start()
+
+    lane = lax.broadcasted_iota(jnp.int32, (rows, HEAD_DIM), 1)
+    row = lax.broadcasted_iota(jnp.int32, (rows, HEAD_DIM), 0)
+
+    def same_request(meta, line):
+        own = jnp.broadcast_to(meta[0:1, :], (rows, HEAD_DIM)).T
+        return own == jnp.broadcast_to(meta[line : line + 1, :], (rows, HEAD_DIM))
+
+    def serve(k, carry):
+        asker = lax.rem(g - k + groups, groups)
+        back = (s, asker, m)
+
+        @pl.when(k > 0)
+        def _():
+            remote(mb.at[asker], mb.at[asker], m_send.at[k], m_recv.at[asker], back).wait_recv()
+            remote(qb.at[asker], qb.at[asker], q_send.at[k], q_recv.at[asker], back).wait_recv()
+
+        seen = same_request(mb[asker].astype(jnp.float32), 1)
+        seen = jnp.where(seen, 1.0, 0.0).astype(jnp.bfloat16)
+        count = jnp.dot(seen, table_ref[asker], preferred_element_type=jnp.float32)
+        facts = jnp.zeros((rows, HEAD_DIM), jnp.float32)
+        for h in range(2):
+            query = qb[asker, :, h * HEAD_DIM : (h + 1) * HEAD_DIM]
+            key = kv_ref[:, h * 2 * HEAD_DIM : h * 2 * HEAD_DIM + HEAD_DIM]
+            value = kv_ref[:, h * 2 * HEAD_DIM + HEAD_DIM : (h + 1) * 2 * HEAD_DIM]
+            scores = jnp.where(count > 0.0, contract_last(query, key) * scale, NEG)
+            top = jnp.max(scores, axis=1, keepdims=True)
+            weight = jnp.exp(scores - top) * count
+            total = jnp.sum(weight, axis=1, keepdims=True)
+            part = jnp.dot(weight.astype(jnp.bfloat16), value, preferred_element_type=jnp.float32)
+            os[asker, :, h * HEAD_DIM : (h + 1) * HEAD_DIM] = part.astype(jnp.bfloat16)
+            facts = jnp.where(lane == 2 * h, top, jnp.where(lane == 2 * h + 1, total, facts))
+        mls[asker] = facts.T[0:8, :]
+
+        @pl.when(k > 0)
+        def _():
+            remote(mls.at[asker], mlr.at[g], l_send.at[k], l_recv.at[g], back).start()
+            remote(os.at[asker], orv.at[g], o_send.at[k], o_recv.at[g], back).start()
+
+        @pl.when(k == 0)
+        def _():
+            mlr[g] = mls[g]
+            orv[g] = os[g]
+
+        return carry
+
+    lax.fori_loop(0, groups, serve, 0)
+
+    visible = same_request(meta_ref[...].astype(jnp.float32), 0) & (lane <= row)
+    fresh = []
+    for h in range(2):
+        base = h * 3 * HEAD_DIM
+        scores = contract_last(qkv_ref[:, base : base + HEAD_DIM], qkv_ref[:, base + HEAD_DIM : base + 2 * HEAD_DIM])
+        scores = jnp.where(visible, scores * scale, NEG)
+        top = jnp.max(scores, axis=1, keepdims=True)
+        weight = jnp.where(visible, jnp.exp(scores - top), 0.0)
+        total = jnp.sum(weight, axis=1, keepdims=True)
+        part = jnp.dot(
+            weight.astype(jnp.bfloat16),
+            qkv_ref[:, base + 2 * HEAD_DIM : base + 3 * HEAD_DIM],
+            preferred_element_type=jnp.float32,
+        )
+        fresh.append((top, total, part))
+
+    def arrive_part(k, carry):
+        owner = lax.rem(g + k, groups)
+        back = (s, owner, m)
+        remote(mls.at[owner], mlr.at[owner], l_send.at[k], l_recv.at[owner], back).wait_recv()
+        remote(os.at[owner], orv.at[owner], o_send.at[k], o_recv.at[owner], back).wait_recv()
+        return carry
+
+    lax.fori_loop(1, groups, arrive_part, 0)
+
+    facts = mlr[...].reshape(groups * 8, HEAD_DIM)
+    facts = jnp.concatenate([facts, jnp.zeros((HEAD_DIM - groups * 8, HEAD_DIM), jnp.float32)], axis=0).T
+    attended = []
+    for h in range(2):
+        top, total, part = fresh[h]
+        best = top
+        for e in range(groups):
+            best = jnp.maximum(best, facts[:, e * 8 + 2 * h : e * 8 + 2 * h + 1])
+        factor = jnp.exp(top - best)
+        mass = factor * total
+        mix = factor * part
+        for e in range(groups):
+            factor = jnp.exp(facts[:, e * 8 + 2 * h : e * 8 + 2 * h + 1] - best)
+            mass = mass + factor * facts[:, e * 8 + 2 * h + 1 : e * 8 + 2 * h + 2]
+            mix = mix + factor * orv[e, :, h * HEAD_DIM : (h + 1) * HEAD_DIM].astype(jnp.float32)
+        attended.append((mix / mass).astype(jnp.bfloat16))
+    attended = jnp.concatenate(attended, axis=1)
+
+    def project(to):
+        cols = pl.ds(pl.multiple_of(to * wide, wide), wide)
+        return jnp.dot(attended, ow_ref[:, cols], preferred_element_type=jnp.float32)
+
+    for j in (1, 3, 2):
+        to = lax.rem(q + j, 4)
+        ps[to] = project(to).astype(jnp.bfloat16)
+        remote(ps.at[to], pr.at[q], p_send.at[j], p_recv.at[q], (to // 2, g, lax.rem(to, 2))).start()
+    mine = pl.ds(pl.multiple_of(q * wide, wide), wide)
+    stream = res_ref[:, mine].astype(jnp.float32) + project(q)
+    for j in (1, 3, 2):
+        at = lax.rem(q + j, 4)
+        remote(ps.at[at], pr.at[at], p_send.at[j], p_recv.at[at], (at // 2, g, lax.rem(at, 2))).wait_recv()
+        stream = stream + pr[at].astype(jnp.float32)
+    mixed[...] = stream
+
+    square = jnp.sum(stream * stream, axis=1, keepdims=True)
+    ss[q] = jnp.broadcast_to(square, (rows, HEAD_DIM)).T[0:8, :]
+    for j in (1, 2, 3):
+        to = lax.rem(q + j, 4)
+        remote(ss.at[q], ss.at[q], s_send.at[j], s_recv.at[q], (to // 2, g, lax.rem(to, 2))).start()
+    for j in (1, 2, 3):
+        at = lax.rem(q + j, 4)
+        remote(ss.at[at], ss.at[at], s_send.at[j], s_recv.at[at], (at // 2, g, lax.rem(at, 2))).wait_recv()
+    square = ss[0] + ss[1] + ss[2] + ss[3]
+    square = jnp.broadcast_to(square[0:1, :], (rows, HEAD_DIM)).T[:, 0:1]
+    inverse = lax.rsqrt(square * (1.0 / (4 * wide)) + 1e-06)
+    nb[...] = (stream * inverse * gain_ref[:, mine]).astype(jnp.bfloat16)
+
+    side = lax.rem(g, 2)
+    place = g // 2
+
+    @pl.when(s == side)
+    def _():
+        xb[place, q] = nb[...]
+
+    @pl.when(s != side)
+    def _():
+        remote(nb, xb.at[place, q], x_send.at[0], x_recv.at[place, q], core_peer).start()
+
+    def dispatch(k, carry):
+        to = (side, lax.rem(g + k, groups), m)
+        remote(nb, xb.at[place, q], x_send.at[k], x_recv.at[place, q], to).start()
+        return carry
+
+    lax.fori_loop(1, groups, dispatch, 0)
+
+    for i, (hbm, vmem) in enumerate(weights):
+        pltpu.make_async_copy(hbm.at[0], vmem.at[s], w_local.at[i]).wait()
+        remote(hbm.at[0], vmem.at[1 - s], w_send.at[i], w_recv.at[i], core_peer).wait()
+
+    first = lax.rem(g + s, 2)
+
+    def slot_of(i):
+        from_group = lax.rem(g - first - 2 * i + 2 * groups, groups)
+        return from_group, from_group // 2
+
+    def forward(i):
+        asker, at = slot_of(i)
+        for c in range(2):
+            piece = 2 * c + m
+
+            @pl.when((asker != g) | (c != s))
+            def _():
+                remote(nb, xb.at[at, piece], x_send.at[0], x_recv.at[at, piece], core_peer).wait_recv()
+
+            remote(xb.at[at, piece], xb.at[at, piece], f_send.at[at, c], x_recv.at[at, piece], x_peer).start()
+
+    def compute(i):
+        asker, at = slot_of(i)
+        for c in range(2):
+            piece = 2 * c + 1 - m
+            remote(xb.at[at, piece], xb.at[at, piece], f_send.at[at, c], x_recv.at[at, piece], x_peer).wait_recv()
+        hidden = []
+        for c in range(2):
+            gate = jnp.zeros((rows, wg.shape[2]), jnp.float32)
+            up = jnp.zeros((rows, wg.shape[2]), jnp.float32)
+            for piece in range(4):
+                rows_in = xb[at, piece]
+                gate += jnp.dot(
+                    rows_in, wg[c, piece * wide : (piece + 1) * wide, :], preferred_element_type=jnp.float32
+                )
+                up += jnp.dot(rows_in, wu[c, piece * wide : (piece + 1) * wide, :], preferred_element_type=jnp.float32)
+            hidden.append((gate / (1.0 + jnp.exp(-gate)) * up).astype(jnp.bfloat16))
+
+        def down(piece):
+            cols = pl.ds(pl.multiple_of(piece * wide, wide), wide)
+            return jnp.dot(hidden[0], wd[0, :, cols], preferred_element_type=jnp.float32) + jnp.dot(
+                hidden[1], wd[1, :, cols], preferred_element_type=jnp.float32
+            )
+
+        for c in range(2):
+            ys[at, c] = down(2 * c + 1 - m).astype(jnp.bfloat16)
+            remote(ys.at[at, c], yr.at[at, c], y_send.at[at, c], y_recv.at[at, c], x_peer).start()
+        for c in range(2):
+            yown[at, c] = down(2 * c + m)
+
+    def give_back(i):
+        asker, at = slot_of(i)
+        for c in range(2):
+            remote(ys.at[at, c], yr.at[at, c], y_send.at[at, c], y_recv.at[at, c], x_peer).wait_recv()
+            rs[at, c] = (yown[at, c] + yr[at, c].astype(jnp.float32)).astype(jnp.bfloat16)
+            is_mine = (asker == g) & (c == s)
+
+            @pl.when(is_mine)
+            def _():
+                rb[g] = rs[at, c]
+
+            @pl.when(jnp.logical_not(is_mine))
+            def _():
+                remote(rs.at[at, c], rb.at[g], r_send.at[at, c], r_recv.at[g], (c, asker, m)).start()
+
+    def step(t, carry):
+        @pl.when(t < half)
+        def _():
+            forward(t)
+
+        @pl.when((t >= 1) & (t <= half))
+        def _():
+            compute(t - 1)
+
+        @pl.when(t >= 2)
+        def _():
+            give_back(t - 2)
+
+        return carry
+
+    lax.fori_loop(0, half + 2, step, 0)
+
+    stream = mixed[...]
+    for e in range(groups):
+
+        @pl.when((e != g) | (s != side))
+        def _():
+            remote(rs.at[0, 0], rb.at[e], r_send.at[0, 0], r_recv.at[e], core_peer).wait_recv()
+
+        stream = stream + cw_ref[:, e : e + 1] * rb[e].astype(jnp.float32)
+    out_ref[...] = stream.astype(jnp.bfloat16)
+
+    def drain(k, carry):
+        to = (s, lax.rem(g + k, groups), m)
+        remote(mb.at[g], mb.at[g], m_send.at[k], m_recv.at[g], to).wait_send()
+        remote(qb.at[g], qb.at[g], q_send.at[k], q_recv.at[g], to).wait_send()
+        remote(mls.at[0], mlr.at[g], l_send.at[k], l_recv.at[g], to).wait_send()
+        remote(os.at[0], orv.at[g], o_send.at[k], o_recv.at[g], to).wait_send()
+        remote(nb, xb.at[place, q], x_send.at[k], x_recv.at[place, q], to).wait_send()
+        return carry
+
+    lax.fori_loop(1, groups, drain, 0)
+
+    @pl.when(s != side)
+    def _():
+        remote(nb, xb.at[place, q], x_send.at[0], x_recv.at[place, q], core_peer).wait_send()
+
+    for j in (1, 2, 3):
+        remote(ps.at[0], pr.at[q], p_send.at[j], p_recv.at[q], core_peer).wait_send()
+        remote(ss.at[q], ss.at[q], s_send.at[j], s_recv.at[q], core_peer).wait_send()
+
+    def drain_slot(i, carry):
+        asker, at = slot_of(i)
+        for c in range(2):
+            remote(xb.at[at, 0], xb.at[at, 0], f_send.at[at, c], x_recv.at[at, 0], x_peer).wait_send()
+            remote(ys.at[at, c], yr.at[at, c], y_send.at[at, c], y_recv.at[at, c], x_peer).wait_send()
+
+            @pl.when((asker != g) | (c != s))
+            def _():
+                remote(rs.at[at, c], rb.at[g], r_send.at[at, c], r_recv.at[g], core_peer).wait_send()
+
+        return carry
+
+    lax.fori_loop(0, half, drain_slot, 0)
+
+
+def local_dense(
+    qkv,
+    kv_cache,
+    residual,
+    out_weight,
+    moe_gain,
+    w_gate,
+    w_up,
+    w_down,
+    seg_ids,
+    prefix_blocks,
+    owners,
+    slot_ids,
+    expert_ids,
+    gate_weights,
+):
+    groups = lax.axis_size("dp")
+    group_index = lax.axis_index("dp")
+    rows = qkv.shape[0]
+    model_width = residual.shape[1]
+    wide = model_width // 4
+    half = groups // 2
+    hid = w_gate.shape[2]
+    slots = kv_cache.shape[0]
+    kv = kv_cache.reshape(slots * BLK, kv_cache.shape[2])
+    block_ends = jnp.cumsum(prefix_blocks[0, 0])
+    block_index = jnp.arange(PREF, dtype=jnp.int32)
+    block_seg = jnp.sum((block_ends[None, :] <= block_index[:, None]).astype(jnp.int32), axis=1)
+    block_seg = jnp.pad(block_seg, (0, HEAD_DIM - PREF), constant_values=-1)
+    meta = jnp.concatenate([seg_ids[0], block_seg[None, :], jnp.zeros((6, HEAD_DIM), jnp.int32)], axis=0)
+    mine = jnp.where(owners[:, 0, :, 0] == group_index, slot_ids[:, 0, :], -1)
+    mine = jnp.pad(mine, ((0, 0), (0, HEAD_DIM - PREF)), constant_values=-1)
+    row_slot = jnp.arange(slots * BLK, dtype=jnp.int32) // BLK
+    table = (mine[:, :, None] == row_slot[None, None, :]).astype(jnp.bfloat16)
+    chosen = expert_ids[:, :, None] == jnp.arange(groups, dtype=jnp.int32)[None, None, :]
+    combine = jnp.sum(jnp.where(chosen, gate_weights[:, :, None], 0.0), axis=1)
+    bf, f32 = jnp.bfloat16, jnp.float32
+    dma = pltpu.SemaphoreType.DMA
+    vmem = pl.BlockSpec(memory_space=pltpu.VMEM)
+    anywhere = pl.BlockSpec(memory_space=pl.ANY)
+    return pl.pallas_call(
+        partial(layer_kernel, groups),
+        out_shape=jax.ShapeDtypeStruct((rows, wide), bf),
+        in_specs=[vmem] * 5 + [anywhere] * 3 + [vmem] * 3,
+        out_specs=vmem,
+        scratch_shapes=[
+            pltpu.VMEM((2, model_width, hid), bf),
+            pltpu.VMEM((2, model_width, hid), bf),
+            pltpu.VMEM((2, hid, model_width), bf),
+            pltpu.VMEM((groups, rows, 2 * HEAD_DIM), bf),
+            pltpu.VMEM((groups, 8, HEAD_DIM), jnp.int32),
+            pltpu.VMEM((groups, rows, 2 * HEAD_DIM), bf),
+            pltpu.VMEM((groups, rows, 2 * HEAD_DIM), bf),
+            pltpu.VMEM((groups, 8, HEAD_DIM), f32),
+            pltpu.VMEM((groups, 8, HEAD_DIM), f32),
+            pltpu.VMEM((4, rows, wide), bf),
+            pltpu.VMEM((4, rows, wide), bf),
+            pltpu.VMEM((4, 8, HEAD_DIM), f32),
+            pltpu.VMEM((rows, wide), bf),
+            pltpu.VMEM((half, 4, rows, wide), bf),
+            pltpu.VMEM((half, 2, rows, wide), f32),
+            pltpu.VMEM((half, 2, rows, wide), bf),
+            pltpu.VMEM((half, 2, rows, wide), bf),
+            pltpu.VMEM((half, 2, rows, wide), bf),
+            pltpu.VMEM((groups, rows, wide), bf),
+            pltpu.VMEM((rows, wide), f32),
+            dma((3,)),
+            dma((3,)),
+            dma((3,)),
+            dma((groups,)),
+            dma((groups,)),
+            dma((groups,)),
+            dma((groups,)),
+            dma((groups,)),
+            dma((groups,)),
+            dma((groups,)),
+            dma((groups,)),
+            dma((4,)),
+            dma((4,)),
+            dma((4,)),
+            dma((4,)),
+            dma((groups,)),
+            dma((half, 4)),
+            dma((half, 2)),
+            dma((half, 2)),
+            dma((half, 2)),
+            dma((half, 2)),
+            dma((groups,)),
+        ],
+        compiler_params=pltpu.CompilerParams(
+            collective_id=0, has_side_effects=True, vmem_limit_bytes=48 * 1024 * 1024
+        ),
+    )(
+        qkv,
+        kv,
+        residual,
+        out_weight,
+        moe_gain.reshape(1, -1),
+        w_gate,
+        w_up,
+        w_down,
+        meta,
+        table,
+        combine,
+    )
+
+
 def solution(mesh):
+    dense = mesh.shape["dp"] <= DENSE_GROUPS
     return jax.shard_map(
-        local,
+        local_dense if dense else local_sparse,
         mesh=mesh,
         in_specs=(
             P("dp", ("section", "mp")),

time: 377 us -> 120 us (0.32)
  waiting for transfers between devices: 183 us -> 0 us
  Pallas kernels: 0 us -> 105 us
  blocking collectives: 97.3 us -> 0 us
  local copies, waits for them, and re-layouts: 30.8 us -> 10.6 us
  matrix products: 19.3 us -> 0 us
  other arithmetic: 17.8 us -> 3.29 us
  between operations: 13.8 us -> 0.04 us
  starting transfers between devices: 11.5 us -> 0 us
    all_to_all x2 -> x0, waiting for transfers between devices: 115 us -> none  [the longest x1 90.1 us: local(): lax.all_to_all(produced, 'dp', split_axis=0, concat_axis=0, tiled=True)]
    pallas_call x0 -> x1, Pallas kernels: none -> 105 us  [local_dense(): pl.pallas_call(partial(layer_kernel, groups), out_shape=jax.ShapeDtypeStr...]
    all_to_all x1 -> x0, blocking collectives: 97.3 us -> none  [local(): lax.all_to_all(outgoing, 'dp', split_axis=0, concat_axis=0, tiled=True)]
    psum x2 -> x0, waiting for transfers between devices: 68.1 us -> none  [the longest x1 35.4 us: local(): mixed_in = stream + lax.psum(projected, ('section', 'mp'))]
    gather x6 -> x0, local copies, waits for them, and re-layouts: 20.9 us -> none  [the longest x2 12.1 us: local(): jnp.take(returned.reshape(groups * capacity, model_width), position, axis=0)]
    dot_general x6 -> x0, matrix products: 19 us -> none  [the longest x1 8.96 us: expert_rows(): jnp.dot(hidden, w_down[0], preferred_element_type=jnp.float32)]
    all_to_all x2 -> x0, starting transfers between devices: 11.2 us -> none  [the longest x1 6.51 us: local(): lax.all_to_all(chosen, 'dp', split_axis=0, concat_axis=0, tiled=True)]
    select_n x8 -> x2, other arithmetic: 5.48 us -> 0.71 us  [the longest x1 0.71 us: local_dense(): mine = jnp.where(owners[:, 0, :, 0] == group_index, slot_ids[:, 0, :], -1)]
  transfers between devices with their start and end apart: 4 -> 0, of which waited for: 4 -> 0; matrix products, arithmetic and copies ran while one was open for 3% -> 0% of each run, Pallas kernels for 0% -> 0%
where the time goes in v1:
time: 120 us; the launch traced here: 119 us
  Pallas kernels  105 us (88%)
  local copies, waits for them, and re-layouts  10.6 us (9%)
  other arithmetic  3.29 us (3%)
    pallas_call x1, Pallas kernels, local_dense(): pl.pallas_call(partial(layer_kernel, groups), out_shape=jax.ShapeDtypeStr...  105 us
    unnamed x17, local copies, waits for them, and re-layouts  9.82 us

profile of v1, /device:TPU:1, one launch (start us, length us, event | category | flops | bytes accessed | tf_op | source)
XLA Modules:
  0.0 119.1 jit_solution(4913340917421087041)
XLA Ops:
  0.0 0.8 reduce-window.8
  0.8 0.1 convert_reduce_fusion
  0.9 0.1 pad.12.clone
  1.0 0.7 add_add_fusion.meta_ref
  1.7 0.7 bitcast_select_fusion
  2.4 0.7 select_reduce_fusion
  3.1 0.7 copy.23.cw_ref
  3.9 0.2 compare_convert_fusion.table_ref
  4.1 2.6 %copy.21.wg_hbm = bf16[1,2048,352]{2,1,0:T(8,128)(2,1)} copy(bf16[1,2048,352]{1,2,0:T(8,128)(2,1)} %param.19) | data formatting | bytes 2883584 | tf_op args[5]
  6.7 0.0 copy-start
  6.7 0.0 copy-start.1
  6.7 0.0 copy-start.6
  6.7 2.7 %copy.22.wu_hbm = bf16[1,2048,352]{2,1,0:T(8,128)(2,1)} copy(bf16[1,2048,352]{1,2,0:T(8,128)(2,1)} %param.20) | data formatting | bytes 2883584 | tf_op args[6]
  9.4 0.0 copy-done
  9.4 0.0 copy-done.1
  9.4 0.0 copy-done.6
  9.4 0.0 copy-start.2
  9.5 1.0 copy-done.2
  10.5 0.0 copy-start.3
  10.5 1.0 copy-done.3
  11.5 0.0 copy-start.4
  11.5 0.8 copy-done.4
  12.4 0.0 copy-start.5
  12.4 0.9 copy-done.5
  13.3 105.2 %shard_map.136 = bf16[128,512]{1,0:T(8,128)(2,1)S(1)} custom-call(bf16[128,768]{1,0:T(8,128)(2,1)S(1)} %copy-done.5, bf16[512,512]{1,0:T(8,128)(2,1)S(1)} %bitcast.11, bf16[128,2048]{1,0:T(8,128)(2,1)S(1)} %copy-done.3, bf16[256,2048]{1,0:T(8,128)(2,1)S(1)} %copy-done.1, f32[1,2048]{1,0:T(1,128)S(1)} %bitcast.12, bf16[1,2048,352]{2,1,0:T(8,128)(2,1)} %copy.21.wg_hbm, ...), custom_call_target="tpu_custom_call" | custom-call | tf_op jit(solution)/shard_map/pallas_call | solution.py:569
  118.5 0.7 copy.25
  (4 shorter events, 0.0 us)
Async XLA Ops:
  6.7 2.7 %copy-start = (bf16[1,352,2048]{2,1,0:T(8,128)(2,1)S(1)}, bf16[1,352,2048]{2,1,0:T(8,128)(2,1)}, u32[]{:S(2)}) copy-start(bf16[1,352,2048]{2,1,0:T(8,128)(2,1)} %wd_hbm.1) | copy-start | bytes 4325380
  6.7 2.7 %copy-start.1 = (bf16[256,2048]{1,0:T(8,128)(2,1)S(1)}, bf16[256,2048]{1,0:T(8,128)(2,1)}, u32[]{:S(2)}) copy-start(bf16[256,2048]{1,0:T(8,128)(2,1)} %ow_ref.1) | copy-start | bytes 3145732
  6.7 2.7 %copy-start.6 = (f32[2048]{0:T(1024)S(1)}, f32[2048]{0:T(1024)}, u32[]{:S(2)}) copy-start(f32[2048]{0:T(1024)} %param.18) | copy-start | bytes 24580
  9.4 1.0 copy-start.2
  10.5 1.0 copy-start.3
  11.5 0.8 copy-start.4
  12.4 0.9 copy-start.5

commit v2 on v1

--- a/solution.py
+++ b/solution.py
@@ -166,18 +166,25 @@
 
 def layer_kernel(
     groups,
+    qkv_hbm,
+    kv_hbm,
+    res_hbm,
+    ow_hbm,
+    gain_ref,
+    wg_hbm,
+    wu_hbm,
+    wd_hbm,
+    seg_ref,
+    count_ref,
+    owner_ref,
+    slot_ref,
+    ids_ref,
+    gates_ref,
+    out_ref,
     qkv_ref,
     kv_ref,
     res_ref,
     ow_ref,
-    gain_ref,
-    wg_hbm,
-    wu_hbm,
-    wd_hbm,
-    meta_ref,
-    table_ref,
-    cw_ref,
-    out_ref,
     wg,
     wu,
     wd,
@@ -198,6 +205,7 @@
     rs,
     rb,
     mixed,
+    in_sem,
     w_local,
     w_send,
     w_recv,
@@ -213,6 +221,7 @@
     p_recv,
     s_send,
     s_recv,
+    n_send,
     x_send,
     x_recv,
     f_send,
@@ -221,13 +230,20 @@
     r_send,
     r_recv,
 ):
+    loads = []
+    for i, (hbm, vmem) in enumerate(((qkv_hbm, qkv_ref), (kv_hbm, kv_ref), (ow_hbm, ow_ref), (res_hbm, res_ref))):
+        loads.append(pltpu.make_async_copy(hbm, vmem, in_sem.at[i]))
+        loads[-1].start()
     s = lax.axis_index("section")
     g = lax.axis_index("dp")
     m = lax.axis_index("mp")
     q = s * 2 + m
+    z, y = g // 2, lax.rem(g, 2)
+    across = g + 1 - 2 * y
     rows = qkv_ref.shape[0]
     wide = out_ref.shape[1]
     half = groups // 2
+    half_line = half // 2
     scale = 1.0 / math.sqrt(HEAD_DIM)
     core_peer = (1 - s, g, m)
     x_peer = (s, g, 1 - m)
@@ -245,43 +261,83 @@
     pl.semaphore_signal(barrier, inc=1, device_id=x_peer, device_id_type=MESH)
     pl.semaphore_signal(barrier, inc=1, device_id=(1 - s, g, 1 - m), device_id_type=MESH)
 
+    def near(i):
+        upper = z // half_line
+        edge = z + upper * (3 - 2 * z)
+        pick = (i // 2) * i + (1 - i // 2) * lax.rem(i + edge, 2)
+        return pick + upper * (3 - 2 * pick)
+
+    def relay(at, piece, sends, recv, sec, mine):
+        @pl.when((at <= z) & (z < half - 1))
+        def _():
+            remote(piece, piece, sends.at[0], recv, (sec, g + 2, mine)).start()
+
+        @pl.when((at >= z) & (z > 0))
+        def _():
+            remote(piece, piece, sends.at[1], recv, (sec, g - 2, mine)).start()
+
+        remote(piece, piece, sends.at[2], recv, (sec, across, mine)).start()
+
+    def relay_done(at, piece, sends, recv):
+        @pl.when((at <= z) & (z < half - 1))
+        def _():
+            remote(piece, piece, sends.at[0], recv, x_peer).wait_send()
+
+        @pl.when((at >= z) & (z > 0))
+        def _():
+            remote(piece, piece, sends.at[1], recv, x_peer).wait_send()
+
+        remote(piece, piece, sends.at[2], recv, x_peer).wait_send()
+
+    lane = lax.broadcasted_iota(jnp.int32, (rows, HEAD_DIM), 1)
+    row = lax.broadcasted_iota(jnp.int32, (rows, HEAD_DIM), 0)
+    ends = count_ref[0, 0]
+    block_seg = jnp.zeros((8, HEAD_DIM), jnp.int32)
+    for r in range(count_ref.shape[1] - 1):
+        block_seg += jnp.where(lane[0:8] >= ends, 1, 0)
+        ends = ends + count_ref[0, r + 1]
+    meta = jnp.where(row[0:8] == 0, jnp.broadcast_to(seg_ref[...], (8, HEAD_DIM)), block_seg)
+    mb[g] = meta
+    loads[0].wait()
     for h in range(2):
         qb[g, :, h * HEAD_DIM : (h + 1) * HEAD_DIM] = qkv_ref[:, h * 3 * HEAD_DIM : h * 3 * HEAD_DIM + HEAD_DIM]
-    mb[g] = meta_ref[...]
     pl.semaphore_wait(barrier, 2 * groups + 1)
 
-    def send_query(k, carry):
-        to = (s, lax.rem(g + k, groups), m)
-        remote(mb.at[g], mb.at[g], m_send.at[k], m_recv.at[g], to).start()
-        remote(qb.at[g], qb.at[g], q_send.at[k], q_recv.at[g], to).start()
-        return carry
-
-    lax.fori_loop(1, groups, send_query, 0)
+    def take_query(src):
+        remote(mb.at[src], mb.at[src], m_send.at[src, 0], m_recv.at[src], x_peer).wait_recv()
+        remote(qb.at[src], qb.at[src], q_send.at[src, 0], q_recv.at[src], x_peer).wait_recv()
+
+    def forward_query(i):
+        at = near(i)
+        src = at * 2 + y
+
+        @pl.when(at != z)
+        def _():
+            take_query(src)
+
+        relay(at, mb.at[src], m_send.at[src], m_recv.at[src], s, m)
+        relay(at, qb.at[src], q_send.at[src], q_recv.at[src], s, m)
+
+    forward_query(0)
 
     weights = ((wg_hbm, wg), (wu_hbm, wu), (wd_hbm, wd))
     for i, (hbm, vmem) in enumerate(weights):
         pltpu.make_async_copy(hbm.at[0], vmem.at[s], w_local.at[i]).start()
         remote(hbm.at[0], vmem.at[s], w_send.at[i], w_recv.at[i], core_peer).start()
 
-    lane = lax.broadcasted_iota(jnp.int32, (rows, HEAD_DIM), 1)
-    row = lax.broadcasted_iota(jnp.int32, (rows, HEAD_DIM), 0)
+    key_slot = lax.broadcasted_iota(jnp.int32, (kv_ref.shape[0], PREF), 0) // BLK
 
     def same_request(meta, line):
         own = jnp.broadcast_to(meta[0:1, :], (rows, HEAD_DIM)).T
         return own == jnp.broadcast_to(meta[line : line + 1, :], (rows, HEAD_DIM))
 
-    def serve(k, carry):
-        asker = lax.rem(g - k + groups, groups)
+    def serve(asker):
         back = (s, asker, m)
-
-        @pl.when(k > 0)
-        def _():
-            remote(mb.at[asker], mb.at[asker], m_send.at[k], m_recv.at[asker], back).wait_recv()
-            remote(qb.at[asker], qb.at[asker], q_send.at[k], q_recv.at[asker], back).wait_recv()
-
         seen = same_request(mb[asker].astype(jnp.float32), 1)
-        seen = jnp.where(seen, 1.0, 0.0).astype(jnp.bfloat16)
-        count = jnp.dot(seen, table_ref[asker], preferred_element_type=jnp.float32)
+        seen = jnp.where(seen, 1.0, 0.0).astype(jnp.bfloat16)[:, :PREF]
+        held = jnp.where(owner_ref[pl.ds(asker, 1), :] == g, slot_ref[pl.ds(asker, 1), :], -1)
+        held = jnp.broadcast_to(held, key_slot.shape) == key_slot
+        count = contract_last(seen, jnp.where(held, 1.0, 0.0).astype(jnp.bfloat16))
         facts = jnp.zeros((rows, HEAD_DIM), jnp.float32)
         for h in range(2):
             query = qb[asker, :, h * HEAD_DIM : (h + 1) * HEAD_DIM]
@@ -296,21 +352,38 @@
             facts = jnp.where(lane == 2 * h, top, jnp.where(lane == 2 * h + 1, total, facts))
         mls[asker] = facts.T[0:8, :]
 
-        @pl.when(k > 0)
-        def _():
-            remote(mls.at[asker], mlr.at[g], l_send.at[k], l_recv.at[g], back).start()
-            remote(os.at[asker], orv.at[g], o_send.at[k], o_recv.at[g], back).start()
-
-        @pl.when(k == 0)
+        @pl.when(asker != g)
+        def _():
+            remote(mls.at[asker], mlr.at[g], l_send.at[asker], l_recv.at[g], back).start()
+            remote(os.at[asker], orv.at[g], o_send.at[asker], o_recv.at[g], back).start()
+
+        @pl.when(asker == g)
         def _():
             mlr[g] = mls[g]
             orv[g] = os[g]
 
+    loads[1].wait()
+
+    def attend_step(t, carry):
+        @pl.when(t < half)
+        def _():
+            forward_query(t)
+
+        @pl.when(t <= half)
+        def _():
+            serve(near(t - 1) * 2 + y)
+
+        @pl.when(t >= 2)
+        def _():
+            src = near(t - 2) * 2 + 1 - y
+            take_query(src)
+            serve(src)
+
         return carry
 
-    lax.fori_loop(0, groups, serve, 0)
-
-    visible = same_request(meta_ref[...].astype(jnp.float32), 0) & (lane <= row)
+    lax.fori_loop(1, half + 2, attend_step, 0)
+
+    visible = same_request(meta.astype(jnp.float32), 0) & (lane <= row)
     fresh = []
     for h in range(2):
         base = h * 3 * HEAD_DIM
@@ -329,8 +402,8 @@
     def arrive_part(k, carry):
         owner = lax.rem(g + k, groups)
         back = (s, owner, m)
-        remote(mls.at[owner], mlr.at[owner], l_send.at[k], l_recv.at[owner], back).wait_recv()
-        remote(os.at[owner], orv.at[owner], o_send.at[k], o_recv.at[owner], back).wait_recv()
+        remote(mls.at[owner], mlr.at[owner], l_send.at[owner], l_recv.at[owner], back).wait_recv()
+        remote(os.at[owner], orv.at[owner], o_send.at[owner], o_recv.at[owner], back).wait_recv()
         return carry
 
     lax.fori_loop(1, groups, arrive_part, 0)
@@ -353,6 +426,8 @@
         attended.append((mix / mass).astype(jnp.bfloat16))
     attended = jnp.concatenate(attended, axis=1)
 
+    loads[2].wait()
+
     def project(to):
         cols = pl.ds(pl.multiple_of(to * wide, wide), wide)
         return jnp.dot(attended, ow_ref[:, cols], preferred_element_type=jnp.float32)
@@ -362,6 +437,7 @@
         ps[to] = project(to).astype(jnp.bfloat16)
         remote(ps.at[to], pr.at[q], p_send.at[j], p_recv.at[q], (to // 2, g, lax.rem(to, 2))).start()
     mine = pl.ds(pl.multiple_of(q * wide, wide), wide)
+    loads[3].wait()
     stream = res_ref[:, mine].astype(jnp.float32) + project(q)
     for j in (1, 3, 2):
         at = lax.rem(q + j, 4)
@@ -382,60 +458,54 @@
     inverse = lax.rsqrt(square * (1.0 / (4 * wide)) + 1e-06)
     nb[...] = (stream * inverse * gain_ref[:, mine]).astype(jnp.bfloat16)
 
-    side = lax.rem(g, 2)
-    place = g // 2
-
-    @pl.when(s == side)
+    @pl.when(s == y)
     def _():
-        xb[place, q] = nb[...]
-
-    @pl.when(s != side)
+        xb[z, q] = nb[...]
+
+    @pl.when(s != y)
     def _():
-        remote(nb, xb.at[place, q], x_send.at[0], x_recv.at[place, q], core_peer).start()
-
-    def dispatch(k, carry):
-        to = (side, lax.rem(g + k, groups), m)
-        remote(nb, xb.at[place, q], x_send.at[k], x_recv.at[place, q], to).start()
-        return carry
-
-    lax.fori_loop(1, groups, dispatch, 0)
+        remote(nb, xb.at[z, q], n_send.at[0], x_recv.at[z, q], core_peer).start()
+
+    @pl.when(s == 1)
+    def _():
+        remote(nb, xb.at[z, q], n_send.at[1], x_recv.at[z, q], (y, g, 1 - m)).start()
 
     for i, (hbm, vmem) in enumerate(weights):
         pltpu.make_async_copy(hbm.at[0], vmem.at[s], w_local.at[i]).wait()
         remote(hbm.at[0], vmem.at[1 - s], w_send.at[i], w_recv.at[i], core_peer).wait()
 
-    first = lax.rem(g + s, 2)
-
     def slot_of(i):
-        from_group = lax.rem(g - first - 2 * i + 2 * groups, groups)
-        return from_group, from_group // 2
+        at = near(i)
+        return at * 2 + s, at
+
+    def take_tokens(at, piece):
+        remote(nb, xb.at[at, piece], n_send.at[0], x_recv.at[at, piece], x_peer).wait_recv()
 
     def forward(i):
         asker, at = slot_of(i)
-        for c in range(2):
-            piece = 2 * c + m
-
-            @pl.when((asker != g) | (c != s))
+        for piece in (m, 2, 3):
+
+            @pl.when((asker != g) | (piece != q))
             def _():
-                remote(nb, xb.at[at, piece], x_send.at[0], x_recv.at[at, piece], core_peer).wait_recv()
-
-            remote(xb.at[at, piece], xb.at[at, piece], f_send.at[at, c], x_recv.at[at, piece], x_peer).start()
+                take_tokens(at, piece)
+
+            @pl.when(s == y)
+            def _():
+                relay(at, xb.at[at, piece], x_send.at[at, piece], x_recv.at[at, piece], s, m)
+
+        remote(xb.at[at, m], xb.at[at, m], f_send.at[at], x_recv.at[at, m], x_peer).start()
 
     def compute(i):
         asker, at = slot_of(i)
-        for c in range(2):
-            piece = 2 * c + 1 - m
-            remote(xb.at[at, piece], xb.at[at, piece], f_send.at[at, c], x_recv.at[at, piece], x_peer).wait_recv()
+        take_tokens(at, 1 - m)
         hidden = []
         for c in range(2):
-            gate = jnp.zeros((rows, wg.shape[2]), jnp.float32)
-            up = jnp.zeros((rows, wg.shape[2]), jnp.float32)
+            gate = jnp.zeros((rows, wg.shape[1]), jnp.float32)
+            up = jnp.zeros((rows, wg.shape[1]), jnp.float32)
             for piece in range(4):
                 rows_in = xb[at, piece]
-                gate += jnp.dot(
-                    rows_in, wg[c, piece * wide : (piece + 1) * wide, :], preferred_element_type=jnp.float32
-                )
-                up += jnp.dot(rows_in, wu[c, piece * wide : (piece + 1) * wide, :], preferred_element_type=jnp.float32)
+                gate += contract_last(rows_in, wg[c, :, piece * wide : (piece + 1) * wide])
+                up += contract_last(rows_in, wu[c, :, piece * wide : (piece + 1) * wide])
             hidden.append((gate / (1.0 + jnp.exp(-gate)) * up).astype(jnp.bfloat16))
 
         def down(piece):
@@ -482,30 +552,37 @@
 
     lax.fori_loop(0, half + 2, step, 0)
 
+    share = jnp.zeros((groups, rows), jnp.float32)
+    expert = lax.broadcasted_iota(jnp.int32, (groups, rows), 0)
+    for k in range(TOPK):
+        named = jnp.broadcast_to(ids_ref[k : k + 1, :], (groups, rows)) == expert
+        share += jnp.where(named, jnp.broadcast_to(gates_ref[k : k + 1, :], (groups, rows)), 0.0)
+    share = jnp.concatenate([share, jnp.zeros((HEAD_DIM - groups, rows), jnp.float32)], axis=0).T
     stream = mixed[...]
     for e in range(groups):
 
-        @pl.when((e != g) | (s != side))
+        @pl.when((e != g) | (s != y))
         def _():
             remote(rs.at[0, 0], rb.at[e], r_send.at[0, 0], r_recv.at[e], core_peer).wait_recv()
 
-        stream = stream + cw_ref[:, e : e + 1] * rb[e].astype(jnp.float32)
+        stream = stream + share[:, e : e + 1] * rb[e].astype(jnp.float32)
     out_ref[...] = stream.astype(jnp.bfloat16)
 
     def drain(k, carry):
-        to = (s, lax.rem(g + k, groups), m)
-        remote(mb.at[g], mb.at[g], m_send.at[k], m_recv.at[g], to).wait_send()
-        remote(qb.at[g], qb.at[g], q_send.at[k], q_recv.at[g], to).wait_send()
-        remote(mls.at[0], mlr.at[g], l_send.at[k], l_recv.at[g], to).wait_send()
-        remote(os.at[0], orv.at[g], o_send.at[k], o_recv.at[g], to).wait_send()
-        remote(nb, xb.at[place, q], x_send.at[k], x_recv.at[place, q], to).wait_send()
+        other = lax.rem(g + k, groups)
+        remote(mls.at[0], mlr.at[g], l_send.at[other], l_recv.at[g], x_peer).wait_send()
+        remote(os.at[0], orv.at[g], o_send.at[other], o_recv.at[g], x_peer).wait_send()
         return carry
 
     lax.fori_loop(1, groups, drain, 0)
 
-    @pl.when(s != side)
+    @pl.when(s != y)
     def _():
-        remote(nb, xb.at[place, q], x_send.at[0], x_recv.at[place, q], core_peer).wait_send()
+        remote(nb, xb.at[z, q], n_send.at[0], x_recv.at[z, q], core_peer).wait_send()
+
+    @pl.when(s == 1)
+    def _():
+        remote(nb, xb.at[z, q], n_send.at[1], x_recv.at[z, q], x_peer).wait_send()
 
     for j in (1, 2, 3):
         remote(ps.at[0], pr.at[q], p_send.at[j], p_recv.at[q], core_peer).wait_send()
@@ -513,8 +590,17 @@
 
     def drain_slot(i, carry):
         asker, at = slot_of(i)
+        src = at * 2 + y
+        relay_done(at, mb.at[src], m_send.at[src], m_recv.at[src])
+        relay_done(at, qb.at[src], q_send.at[src], q_recv.at[src])
+        for piece in (m, 2, 3):
+
+            @pl.when(s == y)
+            def _():
+                relay_done(at, xb.at[at, piece], x_send.at[at, piece], x_recv.at[at, piece])
+
+        remote(xb.at[at, m], xb.at[at, m], f_send.at[at], x_recv.at[at, m], x_peer).wait_send()
         for c in range(2):
-            remote(xb.at[at, 0], xb.at[at, 0], f_send.at[at, c], x_recv.at[at, 0], x_peer).wait_send()
             remote(ys.at[at, c], yr.at[at, c], y_send.at[at, c], y_recv.at[at, c], x_peer).wait_send()
 
             @pl.when((asker != g) | (c != s))
@@ -543,7 +629,6 @@
     gate_weights,
 ):
     groups = lax.axis_size("dp")
-    group_index = lax.axis_index("dp")
     rows = qkv.shape[0]
     model_width = residual.shape[1]
     wide = model_width // 4
@@ -551,29 +636,23 @@
     hid = w_gate.shape[2]
     slots = kv_cache.shape[0]
     kv = kv_cache.reshape(slots * BLK, kv_cache.shape[2])
-    block_ends = jnp.cumsum(prefix_blocks[0, 0])
-    block_index = jnp.arange(PREF, dtype=jnp.int32)
-    block_seg = jnp.sum((block_ends[None, :] <= block_index[:, None]).astype(jnp.int32), axis=1)
-    block_seg = jnp.pad(block_seg, (0, HEAD_DIM - PREF), constant_values=-1)
-    meta = jnp.concatenate([seg_ids[0], block_seg[None, :], jnp.zeros((6, HEAD_DIM), jnp.int32)], axis=0)
-    mine = jnp.where(owners[:, 0, :, 0] == group_index, slot_ids[:, 0, :], -1)
-    mine = jnp.pad(mine, ((0, 0), (0, HEAD_DIM - PREF)), constant_values=-1)
-    row_slot = jnp.arange(slots * BLK, dtype=jnp.int32) // BLK
-    table = (mine[:, :, None] == row_slot[None, None, :]).astype(jnp.bfloat16)
-    chosen = expert_ids[:, :, None] == jnp.arange(groups, dtype=jnp.int32)[None, None, :]
-    combine = jnp.sum(jnp.where(chosen, gate_weights[:, :, None], 0.0), axis=1)
     bf, f32 = jnp.bfloat16, jnp.float32
     dma = pltpu.SemaphoreType.DMA
     vmem = pl.BlockSpec(memory_space=pltpu.VMEM)
+    smem = pl.BlockSpec(memory_space=pltpu.SMEM)
     anywhere = pl.BlockSpec(memory_space=pl.ANY)
     return pl.pallas_call(
         partial(layer_kernel, groups),
         out_shape=jax.ShapeDtypeStruct((rows, wide), bf),
-        in_specs=[vmem] * 5 + [anywhere] * 3 + [vmem] * 3,
+        in_specs=[anywhere] * 4 + [vmem] + [anywhere] * 3 + [vmem, smem, vmem, vmem, vmem, vmem],
         out_specs=vmem,
         scratch_shapes=[
-            pltpu.VMEM((2, model_width, hid), bf),
-            pltpu.VMEM((2, model_width, hid), bf),
+            pltpu.VMEM(qkv.shape, bf),
+            pltpu.VMEM(kv.shape, bf),
+            pltpu.VMEM(residual.shape, bf),
+            pltpu.VMEM(out_weight.shape, bf),
+            pltpu.VMEM((2, hid, model_width), bf),
+            pltpu.VMEM((2, hid, model_width), bf),
             pltpu.VMEM((2, hid, model_width), bf),
             pltpu.VMEM((groups, rows, 2 * HEAD_DIM), bf),
             pltpu.VMEM((groups, 8, HEAD_DIM), jnp.int32),
@@ -592,12 +671,13 @@
             pltpu.VMEM((half, 2, rows, wide), bf),
             pltpu.VMEM((groups, rows, wide), bf),
             pltpu.VMEM((rows, wide), f32),
+            dma((4,)),
             dma((3,)),
             dma((3,)),
             dma((3,)),
+            dma((groups, 3)),
             dma((groups,)),
-            dma((groups,)),
-            dma((groups,)),
+            dma((groups, 3)),
             dma((groups,)),
             dma((groups,)),
             dma((groups,)),
@@ -607,16 +687,17 @@
             dma((4,)),
             dma((4,)),
             dma((4,)),
-            dma((groups,)),
+            dma((2,)),
+            dma((half, 4, 3)),
             dma((half, 4)),
-            dma((half, 2)),
+            dma((half,)),
             dma((half, 2)),
             dma((half, 2)),
             dma((half, 2)),
             dma((groups,)),
         ],
         compiler_params=pltpu.CompilerParams(
-            collective_id=0, has_side_effects=True, vmem_limit_bytes=48 * 1024 * 1024
+            collective_id=0, has_side_effects=True, vmem_limit_bytes=60 * 1024 * 1024
         ),
     )(
         qkv,
@@ -624,12 +705,15 @@
         residual,
         out_weight,
         moe_gain.reshape(1, -1),
-        w_gate,
-        w_up,
+        jnp.swapaxes(w_gate, 1, 2),
+        jnp.swapaxes(w_up, 1, 2),
         w_down,
-        meta,
-        table,
-        combine,
+        seg_ids[0],
+        prefix_blocks[0],
+        owners[:, 0, :, 0],
+        slot_ids[:, 0, :],
+        expert_ids.T,
+        gate_weights.T,
     )
 
 

time: 120 us -> 102 us (0.85)
  local copies, waits for them, and re-layouts: 10.6 us -> 1.57 us
  Pallas kernels: 105 us -> 99.1 us
  other arithmetic: 3.29 us -> 0 us
    unnamed x17 -> x1, local copies, waits for them, and re-layouts: 9.82 us -> 1.57 us
    pallas_call x1, Pallas kernels: 105 us -> 99.1 us  [local_dense(): pl.pallas_call(partial(layer_kernel, groups), out_shape=jax.ShapeDtypeStr...]
where the time goes in v2:
time: 102 us; the launch traced here: 101 us
  Pallas kernels  99.1 us (97%)
  local copies, waits for them, and re-layouts  1.57 us (2%)
    pallas_call x1, Pallas kernels, local_dense(): pl.pallas_call(partial(layer_kernel, groups), out_shape=jax.ShapeDtypeStr...  99.1 us

profile of v2, /device:TPU:1, one launch (start us, length us, event | category | flops | bytes accessed | tf_op | source)
XLA Modules:
  0.0 100.6 jit_solution(6982932257475492128)
XLA Ops:
  0.0 99.1 %shard_map.136 = bf16[128,512]{1,0:T(8,128)(2,1)} custom-call(bf16[128,768]{1,0:T(8,128)(2,1)} %qkv_hbm.1, bf16[512,512]{1,0:T(8,128)(2,1)} %bitcast.12, bf16[128,2048]{1,0:T(8,128)(2,1)} %res_hbm.1, bf16[256,2048]{1,0:T(8,128)(2,1)} %ow_hbm.1, f32[1,2048]{1,0:T(1,128)} %bitcast.13, bf16[1,352,2048]{2,1,0:T(8,128)(2,1)} %bitcast.10, ...), custom_call_target="tpu_custom_call" | custom-call | tf_op jit(solution)/shard_map/pallas_call | solution.py:644
  99.1 1.6 %copy.16 = bf16[128,512]{1,0:T(8,128)(2,1)} copy(bf16[128,512]{1,0:T(8,128)(2,1)} %shard_map.136) | data formatting | bytes 262144

commit v3 on v2

--- a/solution.py
+++ b/solution.py
@@ -188,6 +188,7 @@
     wg,
     wu,
     wd,
+    hb,
     qb,
     mb,
     os,
@@ -320,10 +321,13 @@
 
     forward_query(0)
 
+    hid = wg_hbm.shape[1]
+    own_hidden = pl.ds(pl.multiple_of(s * hid, 16), hid)
+    peer_hidden = pl.ds(pl.multiple_of((1 - s) * hid, 16), hid)
     weights = ((wg_hbm, wg), (wu_hbm, wu), (wd_hbm, wd))
     for i, (hbm, vmem) in enumerate(weights):
-        pltpu.make_async_copy(hbm.at[0], vmem.at[s], w_local.at[i]).start()
-        remote(hbm.at[0], vmem.at[s], w_send.at[i], w_recv.at[i], core_peer).start()
+        pltpu.make_async_copy(hbm.at[0], vmem.at[own_hidden], w_local.at[i]).start()
+        remote(hbm.at[0], vmem.at[own_hidden], w_send.at[i], w_recv.at[i], core_peer).start()
 
     key_slot = lax.broadcasted_iota(jnp.int32, (kv_ref.shape[0], PREF), 0) // BLK
 
@@ -471,8 +475,8 @@
         remote(nb, xb.at[z, q], n_send.at[1], x_recv.at[z, q], (y, g, 1 - m)).start()
 
     for i, (hbm, vmem) in enumerate(weights):
-        pltpu.make_async_copy(hbm.at[0], vmem.at[s], w_local.at[i]).wait()
-        remote(hbm.at[0], vmem.at[1 - s], w_send.at[i], w_recv.at[i], core_peer).wait()
+        pltpu.make_async_copy(hbm.at[0], vmem.at[own_hidden], w_local.at[i]).wait()
+        remote(hbm.at[0], vmem.at[peer_hidden], w_send.at[i], w_recv.at[i], core_peer).wait()
 
     def slot_of(i):
         at = near(i)
@@ -495,30 +499,33 @@
 
         remote(xb.at[at, m], xb.at[at, m], f_send.at[at], x_recv.at[at, m], x_peer).start()
 
-    def compute(i):
-        asker, at = slot_of(i)
-        take_tokens(at, 1 - m)
-        hidden = []
-        for c in range(2):
-            gate = jnp.zeros((rows, wg.shape[1]), jnp.float32)
-            up = jnp.zeros((rows, wg.shape[1]), jnp.float32)
-            for piece in range(4):
-                rows_in = xb[at, piece]
-                gate += contract_last(rows_in, wg[c, :, piece * wide : (piece + 1) * wide])
-                up += contract_last(rows_in, wu[c, :, piece * wide : (piece + 1) * wide])
-            hidden.append((gate / (1.0 + jnp.exp(-gate)) * up).astype(jnp.bfloat16))
-
+    def raise_pair(j):
+        tokens = []
+        for i in range(2):
+            asker, at = slot_of(2 * j + i)
+            take_tokens(at, 1 - m)
+            tokens.append(jnp.concatenate([xb[at, piece] for piece in range(4)], axis=1))
+        tokens = jnp.concatenate(tokens, axis=0)
+        gate = contract_last(tokens, wg[...])
+        up = contract_last(tokens, wu[...])
+        hb[...] = (gate / (1.0 + jnp.exp(-gate)) * up).astype(jnp.bfloat16)
+
+    def lower_pair(j):
         def down(piece):
             cols = pl.ds(pl.multiple_of(piece * wide, wide), wide)
-            return jnp.dot(hidden[0], wd[0, :, cols], preferred_element_type=jnp.float32) + jnp.dot(
-                hidden[1], wd[1, :, cols], preferred_element_type=jnp.float32
-            )
+            return jnp.dot(hb[...], wd[:, cols], preferred_element_type=jnp.float32)
 
         for c in range(2):
-            ys[at, c] = down(2 * c + 1 - m).astype(jnp.bfloat16)
-            remote(ys.at[at, c], yr.at[at, c], y_send.at[at, c], y_recv.at[at, c], x_peer).start()
+            result = down(2 * c + 1 - m).astype(jnp.bfloat16)
+            for i in range(2):
+                asker, at = slot_of(2 * j + i)
+                ys[at, c] = result[i * rows : (i + 1) * rows]
+                remote(ys.at[at, c], yr.at[at, c], y_send.at[at, c], y_recv.at[at, c], x_peer).start()
         for c in range(2):
-            yown[at, c] = down(2 * c + m)
+            result = down(2 * c + m)
+            for i in range(2):
+                asker, at = slot_of(2 * j + i)
+                yown[at, c] = result[i * rows : (i + 1) * rows]
 
     def give_back(i):
         asker, at = slot_of(i)
@@ -535,22 +542,36 @@
             def _():
                 remote(rs.at[at, c], rb.at[g], r_send.at[at, c], r_recv.at[g], (c, asker, m)).start()
 
-    def step(t, carry):
-        @pl.when(t < half)
-        def _():
-            forward(t)
-
-        @pl.when((t >= 1) & (t <= half))
-        def _():
-            compute(t - 1)
-
-        @pl.when(t >= 2)
-        def _():
-            give_back(t - 2)
+    pairs = half // 2
+    forward(0)
+    forward(1)
+
+    def step(j, carry):
+        raise_pair(j)
+
+        @pl.when(j < pairs - 1)
+        def _():
+            forward(2 * j + 2)
+
+        @pl.when(j > 0)
+        def _():
+            give_back(2 * j - 2)
+
+        lower_pair(j)
+
+        @pl.when(j < pairs - 1)
+        def _():
+            forward(2 * j + 3)
+
+        @pl.when(j > 0)
+        def _():
+            give_back(2 * j - 1)
 
         return carry
 
-    lax.fori_loop(0, half + 2, step, 0)
+    lax.fori_loop(0, pairs, step, 0)
+    give_back(half - 2)
+    give_back(half - 1)
 
     share = jnp.zeros((groups, rows), jnp.float32)
     expert = lax.broadcasted_iota(jnp.int32, (groups, rows), 0)
@@ -651,9 +672,10 @@
             pltpu.VMEM(kv.shape, bf),
             pltpu.VMEM(residual.shape, bf),
             pltpu.VMEM(out_weight.shape, bf),
-            pltpu.VMEM((2, hid, model_width), bf),
-            pltpu.VMEM((2, hid, model_width), bf),
-            pltpu.VMEM((2, hid, model_width), bf),
+            pltpu.VMEM((2 * hid, model_width), bf),
+            pltpu.VMEM((2 * hid, model_width), bf),
+            pltpu.VMEM((2 * hid, model_width), bf),
+            pltpu.VMEM((2 * rows, 2 * hid), bf),
             pltpu.VMEM((groups, rows, 2 * HEAD_DIM), bf),
             pltpu.VMEM((groups, 8, HEAD_DIM), jnp.int32),
             pltpu.VMEM((groups, rows, 2 * HEAD_DIM), bf),

time: 102 us -> 105 us (1.029); the launches traced: 101 us -> 105 us
  Pallas kernels: 99.1 us -> 104 us
    pallas_call x1, Pallas kernels: 99.1 us -> 104 us  [local_dense(): pl.pallas_call(partial(layer_kernel, groups), out_shape=jax.ShapeDtypeStr...]
where the time goes in v3:
time: 105 us
  Pallas kernels  104 us (99%)
  local copies, waits for them, and re-layouts  1.57 us (1%)
    pallas_call x1, Pallas kernels, local_dense(): pl.pallas_call(partial(layer_kernel, groups), out_shape=jax.ShapeDtypeStr...  104 us

profile of v3, /device:TPU:1, one launch (start us, length us, event | category | flops | bytes accessed | tf_op | source)
XLA Modules:
  0.0 105.1 jit_solution(14815118989484951886)
XLA Ops:
  0.0 103.5 %shard_map.136 = bf16[128,512]{1,0:T(8,128)(2,1)} custom-call(bf16[128,768]{1,0:T(8,128)(2,1)} %qkv_hbm.1, bf16[512,512]{1,0:T(8,128)(2,1)} %bitcast.12, bf16[128,2048]{1,0:T(8,128)(2,1)} %res_hbm.1, bf16[256,2048]{1,0:T(8,128)(2,1)} %ow_hbm.1, f32[1,2048]{1,0:T(1,128)} %bitcast.13, bf16[1,352,2048]{2,1,0:T(8,128)(2,1)} %bitcast.10, ...), custom_call_target="tpu_custom_call" | custom-call | tf_op jit(solution)/shard_map/pallas_call | solution.py:665
  103.6 1.6 %copy.16 = bf16[128,512]{1,0:T(8,128)(2,1)} copy(bf16[128,512]{1,0:T(8,128)(2,1)} %shard_map.136) | data formatting | bytes 262144

commit v4 on v2

--- a/solution.py
+++ b/solution.py
@@ -320,10 +320,12 @@
 
     forward_query(0)
 
+    hid = wg_hbm.shape[1]
+    own_hidden = pl.ds(pl.multiple_of(s * hid, 16), hid)
+    peer_hidden = pl.ds(pl.multiple_of((1 - s) * hid, 16), hid)
     weights = ((wg_hbm, wg), (wu_hbm, wu), (wd_hbm, wd))
     for i, (hbm, vmem) in enumerate(weights):
-        pltpu.make_async_copy(hbm.at[0], vmem.at[s], w_local.at[i]).start()
-        remote(hbm.at[0], vmem.at[s], w_send.at[i], w_recv.at[i], core_peer).start()
+        pltpu.make_async_copy(hbm.at[0], vmem.at[own_hidden], w_local.at[i]).start()
 
     key_slot = lax.broadcasted_iota(jnp.int32, (kv_ref.shape[0], PREF), 0) // BLK
 
@@ -379,6 +381,12 @@
             take_query(src)
             serve(src)
 
+        for i, (hbm, vmem) in enumerate(weights):
+
+            @pl.when(t == i + 2)
+            def _():
+                remote(hbm.at[0], vmem.at[own_hidden], w_send.at[i], w_recv.at[i], core_peer).start()
+
         return carry
 
     lax.fori_loop(1, half + 2, attend_step, 0)
@@ -471,8 +479,8 @@
         remote(nb, xb.at[z, q], n_send.at[1], x_recv.at[z, q], (y, g, 1 - m)).start()
 
     for i, (hbm, vmem) in enumerate(weights):
-        pltpu.make_async_copy(hbm.at[0], vmem.at[s], w_local.at[i]).wait()
-        remote(hbm.at[0], vmem.at[1 - s], w_send.at[i], w_recv.at[i], core_peer).wait()
+        pltpu.make_async_copy(hbm.at[0], vmem.at[own_hidden], w_local.at[i]).wait()
+        remote(hbm.at[0], vmem.at[peer_hidden], w_send.at[i], w_recv.at[i], core_peer).wait()
 
     def slot_of(i):
         at = near(i)
@@ -489,30 +497,25 @@
             def _():
                 take_tokens(at, piece)
 
+            if piece is m:
+                remote(xb.at[at, m], xb.at[at, m], f_send.at[at], x_recv.at[at, m], x_peer).start()
+
             @pl.when(s == y)
             def _():
                 relay(at, xb.at[at, piece], x_send.at[at, piece], x_recv.at[at, piece], s, m)
 
-        remote(xb.at[at, m], xb.at[at, m], f_send.at[at], x_recv.at[at, m], x_peer).start()
 
     def compute(i):
         asker, at = slot_of(i)
         take_tokens(at, 1 - m)
-        hidden = []
-        for c in range(2):
-            gate = jnp.zeros((rows, wg.shape[1]), jnp.float32)
-            up = jnp.zeros((rows, wg.shape[1]), jnp.float32)
-            for piece in range(4):
-                rows_in = xb[at, piece]
-                gate += contract_last(rows_in, wg[c, :, piece * wide : (piece + 1) * wide])
-                up += contract_last(rows_in, wu[c, :, piece * wide : (piece + 1) * wide])
-            hidden.append((gate / (1.0 + jnp.exp(-gate)) * up).astype(jnp.bfloat16))
+        tokens = jnp.concatenate([xb[at, piece] for piece in range(4)], axis=1)
+        gate = contract_last(tokens, wg[...])
+        up = contract_last(tokens, wu[...])
+        hidden = (gate / (1.0 + jnp.exp(-gate)) * up).astype(jnp.bfloat16)
 
         def down(piece):
             cols = pl.ds(pl.multiple_of(piece * wide, wide), wide)
-            return jnp.dot(hidden[0], wd[0, :, cols], preferred_element_type=jnp.float32) + jnp.dot(
-                hidden[1], wd[1, :, cols], preferred_element_type=jnp.float32
-            )
+            return jnp.dot(hidden, wd[:, cols], preferred_element_type=jnp.float32)
 
         for c in range(2):
             ys[at, c] = down(2 * c + 1 - m).astype(jnp.bfloat16)
@@ -651,9 +654,9 @@
             pltpu.VMEM(kv.shape, bf),
             pltpu.VMEM(residual.shape, bf),
             pltpu.VMEM(out_weight.shape, bf),
-            pltpu.VMEM((2, hid, model_width), bf),
-            pltpu.VMEM((2, hid, model_width), bf),
-            pltpu.VMEM((2, hid, model_width), bf),
+            pltpu.VMEM((2 * hid, model_width), bf),
+            pltpu.VMEM((2 * hid, model_width), bf),
+            pltpu.VMEM((2 * hid, model_width), bf),
             pltpu.VMEM((groups, rows, 2 * HEAD_DIM), bf),
             pltpu.VMEM((groups, 8, HEAD_DIM), jnp.int32),
             pltpu.VMEM((groups, rows, 2 * HEAD_DIM), bf),

time: 102 us -> 99.9 us (0.979)
  Pallas kernels: 99.1 us -> 97.6 us
    pallas_call x1, Pallas kernels: 99.1 us -> 97.6 us  [local_dense(): pl.pallas_call(partial(layer_kernel, groups), out_shape=jax.ShapeDtypeStr...]
where the time goes in v4:
time: 99.9 us; the launch traced here: 99.2 us
  Pallas kernels  97.6 us (98%)
  local copies, waits for them, and re-layouts  1.57 us (2%)
    pallas_call x1, Pallas kernels, local_dense(): pl.pallas_call(partial(layer_kernel, groups), out_shape=jax.ShapeDtypeStr...  97.6 us

profile of v4, /device:TPU:1, one launch (start us, length us, event | category | flops | bytes accessed | tf_op | source)
XLA Modules:
  0.0 99.2 jit_solution(11480420395380066185)
XLA Ops:
  0.0 97.6 %shard_map.136 = bf16[128,512]{1,0:T(8,128)(2,1)} custom-call(bf16[128,768]{1,0:T(8,128)(2,1)} %qkv_hbm.1, bf16[512,512]{1,0:T(8,128)(2,1)} %bitcast.12, bf16[128,2048]{1,0:T(8,128)(2,1)} %res_hbm.1, bf16[256,2048]{1,0:T(8,128)(2,1)} %ow_hbm.1, f32[1,2048]{1,0:T(1,128)} %bitcast.13, bf16[1,352,2048]{2,1,0:T(8,128)(2,1)} %bitcast.10, ...), custom_call_target="tpu_custom_call" | custom-call | tf_op jit(solution)/shard_map/pallas_call | solution.py:647
  97.6 1.6 %copy.16 = bf16[128,512]{1,0:T(8,128)(2,1)} copy(bf16[128,512]{1,0:T(8,128)(2,1)} %shard_map.136) | data formatting | bytes 262144

commit v5 on v4

--- a/solution.py
+++ b/solution.py
@@ -202,6 +202,8 @@
     yown,
     ys,
     yr,
+    vs,
+    vr,
     rs,
     rb,
     mixed,
@@ -227,6 +229,8 @@
     f_send,
     y_send,
     y_recv,
+    v_send,
+    v_recv,
     r_send,
     r_recv,
 ):
@@ -297,7 +301,13 @@
         block_seg += jnp.where(lane[0:8] >= ends, 1, 0)
         ends = ends + count_ref[0, r + 1]
     meta = jnp.where(row[0:8] == 0, jnp.broadcast_to(seg_ref[...], (8, HEAD_DIM)), block_seg)
-    mb[g] = meta
+    meta = meta.astype(jnp.float32)
+    share = jnp.zeros((groups, rows), jnp.float32)
+    expert = lax.broadcasted_iota(jnp.int32, (groups, rows), 0)
+    for k in range(TOPK):
+        named = jnp.broadcast_to(ids_ref[k : k + 1, :], (groups, rows)) == expert
+        share += jnp.where(named, jnp.broadcast_to(gates_ref[k : k + 1, :], (groups, rows)), 0.0)
+    mb[g] = jnp.concatenate([meta, share], axis=0)
     loads[0].wait()
     for h in range(2):
         qb[g, :, h * HEAD_DIM : (h + 1) * HEAD_DIM] = qkv_ref[:, h * 3 * HEAD_DIM : h * 3 * HEAD_DIM + HEAD_DIM]
@@ -335,7 +345,7 @@
 
     def serve(asker):
         back = (s, asker, m)
-        seen = same_request(mb[asker].astype(jnp.float32), 1)
+        seen = same_request(mb[asker], 1)
         seen = jnp.where(seen, 1.0, 0.0).astype(jnp.bfloat16)[:, :PREF]
         held = jnp.where(owner_ref[pl.ds(asker, 1), :] == g, slot_ref[pl.ds(asker, 1), :], -1)
         held = jnp.broadcast_to(held, key_slot.shape) == key_slot
@@ -391,7 +401,7 @@
 
     lax.fori_loop(1, half + 2, attend_step, 0)
 
-    visible = same_request(meta.astype(jnp.float32), 0) & (lane <= row)
+    visible = same_request(meta, 0) & (lane <= row)
     fresh = []
     for h in range(2):
         base = h * 3 * HEAD_DIM
@@ -505,6 +515,12 @@
                 relay(at, xb.at[at, piece], x_send.at[at, piece], x_recv.at[at, piece], s, m)
 
 
+    def pass_on(at, k):
+        return remote(vs.at[at, k], vr.at[at, k], v_send.at[at, k], v_recv.at[at, k], (s, across, m))
+
+    def trade(at, c):
+        return remote(ys.at[at, c], yr.at[at, c], y_send.at[at, c], y_recv.at[at, c], x_peer)
+
     def compute(i):
         asker, at = slot_of(i)
         take_tokens(at, 1 - m)
@@ -513,30 +529,62 @@
         up = contract_last(tokens, wu[...])
         hidden = (gate / (1.0 + jnp.exp(-gate)) * up).astype(jnp.bfloat16)
 
+        weight = jnp.broadcast_to(mb[asker, pl.ds(8 + g, 1), :], (rows, HEAD_DIM)).T[:, 0:1]
+
         def down(piece):
             cols = pl.ds(pl.multiple_of(piece * wide, wide), wide)
-            return jnp.dot(hidden, wd[:, cols], preferred_element_type=jnp.float32)
-
-        for c in range(2):
-            ys[at, c] = down(2 * c + 1 - m).astype(jnp.bfloat16)
-            remote(ys.at[at, c], yr.at[at, c], y_send.at[at, c], y_recv.at[at, c], x_peer).start()
-        for c in range(2):
-            yown[at, c] = down(2 * c + m)
+            return jnp.dot(hidden, wd[:, cols], preferred_element_type=jnp.float32) * weight
+
+        for k in (1, 2):
+            yown[at, k] = down(k + 1)
+
+        @pl.when(s != y)
+        def _():
+            for k in (1, 2):
+                vs[at, k] = yown[at, k].astype(jnp.bfloat16)
+                pass_on(at, k).start()
+
+        ys[at, 0] = down(1 - m).astype(jnp.bfloat16)
+        trade(at, 0).start()
+        yown[at, 0] = down(m)
+
+    def gather_half(i):
+        asker, at = slot_of(i)
+        trade(at, 0).wait_recv()
+        yown[at, 0] = yown[at, 0] + yr[at, 0].astype(jnp.float32)
+
+        @pl.when(s != y)
+        def _():
+            vs[at, 0] = yown[at, 0].astype(jnp.bfloat16)
+            pass_on(at, 0).start()
+
+        @pl.when(s == y)
+        def _():
+            for k in (1, 2):
+                pass_on(at, k).wait_recv()
+                yown[at, k] = yown[at, k] + vr[at, k].astype(jnp.float32)
+            ys[at, 1] = yown[at, 2 - m].astype(jnp.bfloat16)
+            trade(at, 1).start()
 
     def give_back(i):
         asker, at = slot_of(i)
         for c in range(2):
-            remote(ys.at[at, c], yr.at[at, c], y_send.at[at, c], y_recv.at[at, c], x_peer).wait_recv()
-            rs[at, c] = (yown[at, c] + yr[at, c].astype(jnp.float32)).astype(jnp.bfloat16)
+            if c == 0:
+                pass_on(at, 0).wait_recv()
+                total = yown[at, 0] + vr[at, 0].astype(jnp.float32)
+            else:
+                trade(at, 1).wait_recv()
+                total = yown[at, 1 + m] + yr[at, 1].astype(jnp.float32)
+            rs[at, c] = total.astype(jnp.bfloat16)
             is_mine = (asker == g) & (c == s)
 
             @pl.when(is_mine)
             def _():
-                rb[g] = rs[at, c]
+                rb[z] = rs[at, c]
 
             @pl.when(jnp.logical_not(is_mine))
             def _():
-                remote(rs.at[at, c], rb.at[g], r_send.at[at, c], r_recv.at[g], (c, asker, m)).start()
+                remote(rs.at[at, c], rb.at[z], r_send.at[at, c], r_recv.at[z], (c, asker, m)).start()
 
     def step(t, carry):
         @pl.when(t < half)
@@ -547,28 +595,26 @@
         def _():
             compute(t - 1)
 
-        @pl.when(t >= 2)
-        def _():
-            give_back(t - 2)
+        @pl.when((t >= 2) & (t <= half + 1))
+        def _():
+            gather_half(t - 2)
+
+        @pl.when((t >= 3) & (s == y))
+        def _():
+            give_back(t - 3)
 
         return carry
 
-    lax.fori_loop(0, half + 2, step, 0)
-
-    share = jnp.zeros((groups, rows), jnp.float32)
-    expert = lax.broadcasted_iota(jnp.int32, (groups, rows), 0)
-    for k in range(TOPK):
-        named = jnp.broadcast_to(ids_ref[k : k + 1, :], (groups, rows)) == expert
-        share += jnp.where(named, jnp.broadcast_to(gates_ref[k : k + 1, :], (groups, rows)), 0.0)
-    share = jnp.concatenate([share, jnp.zeros((HEAD_DIM - groups, rows), jnp.float32)], axis=0).T
+    lax.fori_loop(0, half + 3, step, 0)
+
     stream = mixed[...]
-    for e in range(groups):
-
-        @pl.when((e != g) | (s != y))
+    for e in range(half):
+
+        @pl.when((e != z) | (s != y))
         def _():
             remote(rs.at[0, 0], rb.at[e], r_send.at[0, 0], r_recv.at[e], core_peer).wait_recv()
 
-        stream = stream + share[:, e : e + 1] * rb[e].astype(jnp.float32)
+        stream = stream + rb[e].astype(jnp.float32)
     out_ref[...] = stream.astype(jnp.bfloat16)
 
     def drain(k, carry):
@@ -603,12 +649,21 @@
                 relay_done(at, xb.at[at, piece], x_send.at[at, piece], x_recv.at[at, piece])
 
         remote(xb.at[at, m], xb.at[at, m], f_send.at[at], x_recv.at[at, m], x_peer).wait_send()
-        for c in range(2):
-            remote(ys.at[at, c], yr.at[at, c], y_send.at[at, c], y_recv.at[at, c], x_peer).wait_send()
-
-            @pl.when((asker != g) | (c != s))
-            def _():
-                remote(rs.at[at, c], rb.at[g], r_send.at[at, c], r_recv.at[g], core_peer).wait_send()
+        trade(at, 0).wait_send()
+
+        @pl.when(s != y)
+        def _():
+            for k in range(3):
+                pass_on(at, k).wait_send()
+
+        @pl.when(s == y)
+        def _():
+            trade(at, 1).wait_send()
+            for c in range(2):
+
+                @pl.when((asker != g) | (c != s))
+                def _():
+                    remote(rs.at[at, c], rb.at[z], r_send.at[at, c], r_recv.at[z], core_peer).wait_send()
 
         return carry
 
@@ -658,7 +713,7 @@
             pltpu.VMEM((2 * hid, model_width), bf),
             pltpu.VMEM((2 * hid, model_width), bf),
             pltpu.VMEM((groups, rows, 2 * HEAD_DIM), bf),
-            pltpu.VMEM((groups, 8, HEAD_DIM), jnp.int32),
+            pltpu.VMEM((groups, 8 + groups, HEAD_DIM), f32),
             pltpu.VMEM((groups, rows, 2 * HEAD_DIM), bf),
             pltpu.VMEM((groups, rows, 2 * HEAD_DIM), bf),
             pltpu.VMEM((groups, 8, HEAD_DIM), f32),
@@ -668,11 +723,13 @@
             pltpu.VMEM((4, 8, HEAD_DIM), f32),
             pltpu.VMEM((rows, wide), bf),
             pltpu.VMEM((half, 4, rows, wide), bf),
-            pltpu.VMEM((half, 2, rows, wide), f32),
+            pltpu.VMEM((half, 3, rows, wide), f32),
             pltpu.VMEM((half, 2, rows, wide), bf),
             pltpu.VMEM((half, 2, rows, wide), bf),
+            pltpu.VMEM((half, 3, rows, wide), bf),
+            pltpu.VMEM((half, 3, rows, wide), bf),
             pltpu.VMEM((half, 2, rows, wide), bf),
-            pltpu.VMEM((groups, rows, wide), bf),
+            pltpu.VMEM((half, rows, wide), bf),
             pltpu.VMEM((rows, wide), f32),
             dma((4,)),
             dma((3,)),
@@ -696,8 +753,10 @@
             dma((half,)),
             dma((half, 2)),
             dma((half, 2)),
+            dma((half, 3)),
+            dma((half, 3)),
             dma((half, 2)),
-            dma((groups,)),
+            dma((half,)),
         ],
         compiler_params=pltpu.CompilerParams(
             collective_id=0, has_side_effects=True, vmem_limit_bytes=60 * 1024 * 1024

time: 99.9 us -> 100 us (level)
  no operation moved by 1% of the time
where the time goes in v5:
time: 100 us; the launch traced here: 99.9 us
  Pallas kernels  98.3 us (98%)
  local copies, waits for them, and re-layouts  1.57 us (2%)
    pallas_call x1, Pallas kernels, local_dense(): pl.pallas_call(partial(layer_kernel, groups), out_shape=jax.ShapeDtypeStr...  98.3 us

profile of v5, /device:TPU:1, one launch (start us, length us, event | category | flops | bytes accessed | tf_op | source)
XLA Modules:
  0.0 99.9 jit_solution(1158146198001712539)
XLA Ops:
  0.0 98.3 %shard_map.136 = bf16[128,512]{1,0:T(8,128)(2,1)} custom-call(bf16[128,768]{1,0:T(8,128)(2,1)} %qkv_hbm.1, bf16[512,512]{1,0:T(8,128)(2,1)} %bitcast.12, bf16[128,2048]{1,0:T(8,128)(2,1)} %res_hbm.1, bf16[256,2048]{1,0:T(8,128)(2,1)} %ow_hbm.1, f32[1,2048]{1,0:T(1,128)} %bitcast.13, bf16[1,352,2048]{2,1,0:T(8,128)(2,1)} %bitcast.10, ...), custom_call_target="tpu_custom_call" | custom-call | tf_op jit(solution)/shard_map/pallas_call | solution.py:702
  98.3 1.6 %copy.16 = bf16[128,512]{1,0:T(8,128)(2,1)} copy(bf16[128,512]{1,0:T(8,128)(2,1)} %shard_map.136) | data formatting | bytes 262144

commit v6 on v4

--- a/solution.py
+++ b/solution.py
@@ -340,14 +340,15 @@
         held = jnp.where(owner_ref[pl.ds(asker, 1), :] == g, slot_ref[pl.ds(asker, 1), :], -1)
         held = jnp.broadcast_to(held, key_slot.shape) == key_slot
         count = contract_last(seen, jnp.where(held, 1.0, 0.0).astype(jnp.bfloat16))
+        bias = jnp.where(count > 0.0, jnp.log(jnp.maximum(count, 1.0)), NEG)
         facts = jnp.zeros((rows, HEAD_DIM), jnp.float32)
         for h in range(2):
             query = qb[asker, :, h * HEAD_DIM : (h + 1) * HEAD_DIM]
             key = kv_ref[:, h * 2 * HEAD_DIM : h * 2 * HEAD_DIM + HEAD_DIM]
             value = kv_ref[:, h * 2 * HEAD_DIM + HEAD_DIM : (h + 1) * 2 * HEAD_DIM]
-            scores = jnp.where(count > 0.0, contract_last(query, key) * scale, NEG)
+            scores = contract_last(query, key) * scale + bias
             top = jnp.max(scores, axis=1, keepdims=True)
-            weight = jnp.exp(scores - top) * count
+            weight = jnp.exp(scores - top)
             total = jnp.sum(weight, axis=1, keepdims=True)
             part = jnp.dot(weight.astype(jnp.bfloat16), value, preferred_element_type=jnp.float32)
             os[asker, :, h * HEAD_DIM : (h + 1) * HEAD_DIM] = part.astype(jnp.bfloat16)
@@ -425,10 +426,11 @@
         for e in range(groups):
             best = jnp.maximum(best, facts[:, e * 8 + 2 * h : e * 8 + 2 * h + 1])
         factor = jnp.exp(top - best)
+        factors = jnp.exp(facts - best)
         mass = factor * total
         mix = factor * part
         for e in range(groups):
-            factor = jnp.exp(facts[:, e * 8 + 2 * h : e * 8 + 2 * h + 1] - best)
+            factor = factors[:, e * 8 + 2 * h : e * 8 + 2 * h + 1]
             mass = mass + factor * facts[:, e * 8 + 2 * h + 1 : e * 8 + 2 * h + 2]
             mix = mix + factor * orv[e, :, h * HEAD_DIM : (h + 1) * HEAD_DIM].astype(jnp.float32)
         attended.append((mix / mass).astype(jnp.bfloat16))

time: 99.9 us -> 99 us (level)
  Pallas kernels: 97.6 us -> 96.6 us
where the time goes in v6:
time: 99 us; the launch traced here: 98.2 us
  Pallas kernels  96.6 us (98%)
  local copies, waits for them, and re-layouts  1.57 us (2%)
    pallas_call x1, Pallas kernels, local_dense(): pl.pallas_call(partial(layer_kernel, groups), out_shape=jax.ShapeDtypeStr...  96.6 us

profile of v6, /device:TPU:1, one launch (start us, length us, event | category | flops | bytes accessed | tf_op | source)
XLA Modules:
  0.0 98.2 jit_solution(16691661994283063737)
XLA Ops:
  0.0 96.6 %shard_map.136 = bf16[128,512]{1,0:T(8,128)(2,1)} custom-call(bf16[128,768]{1,0:T(8,128)(2,1)} %qkv_hbm.1, bf16[512,512]{1,0:T(8,128)(2,1)} %bitcast.12, bf16[128,2048]{1,0:T(8,128)(2,1)} %res_hbm.1, bf16[256,2048]{1,0:T(8,128)(2,1)} %ow_hbm.1, f32[1,2048]{1,0:T(1,128)} %bitcast.13, bf16[1,352,2048]{2,1,0:T(8,128)(2,1)} %bitcast.10, ...), custom_call_target="tpu_custom_call" | custom-call | tf_op jit(solution)/shard_map/pallas_call | solution.py:649
  96.6 1.6 %copy.16 = bf16[128,512]{1,0:T(8,128)(2,1)} copy(bf16[128,512]{1,0:T(8,128)(2,1)} %shard_map.136) | data formatting | bytes 262144
